TPU v7x, 32 devices: a whole 2x2x4 slice. The times are simulated.
32 devices in a mesh: case: 2 (over y), ax: 16 (over z, x, core).
Axes of the slice: x: 2, y: 2, z: 4, core: 2. Of those that a mesh axis runs over, the one named last changes fastest.
Arguments:
- checkpoint: float32 [32, 384, 1536], P(('case', 'ax')), parts along dimension 0, may hold values from -6 to 6
- cotangent: float32 [32, 384, 1536], P(('case', 'ax')), parts along dimension 0, may hold values from -6 to 6
- amplitudes: float32 [512], P('case'), parts along dimension 0, may hold values from -6 to 6
- patch_ids: int32 [32, 1536], P(('case', 'ax')), parts along dimension 0, may hold values from 0 to 255
- substep: int32 [2], P('case'), parts along dimension 0, may hold values from 0 to 2
- axial_speed: float32 [384], replicated, may hold values from 0.5 to 1.5
- radial_diffusion: float32 [384], replicated, may hold values from 0.05 to 0.3
- azimuth_diffusion: float32 [384], replicated, may hold values from 0.05 to 0.3
Outputs:
- advanced: float32 [32, 384, 1536], P(('case', 'ax')), parts along dimension 0
- adjoint_state: float32 [32, 384, 1536], P(('case', 'ax')), parts along dimension 0
- actuation_grad: float32 [512], P('case'), parts along dimension 0
There are 2 independent parts, one for each index of `case`. A program takes and returns all parts, laid end to end along the dimension named above; an argument that names none is the same for every part. Nothing has to cross between parts.
All inputs are finite; a program needn't handle non-finite values.
Results may differ from a plain program's by a relative error of at most 0.00002.
Values sent between devices are 32-bit elements; how exact they have to be, the bound alone decides.
No kernel may reach another device: no remote copies, remote signals or barrier semaphores. Data moves between devices by JAX's collectives and lax.ppermute only.
A program may use at most 64 MiB of HBM per device.

v0:
```python
import jax
import jax.numpy as jnp
from jax import lax
from jax.sharding import PartitionSpec as P

time_step = 0.6
dissipation = 2.0


def with_halo(value, sides, width):
    for axis, dim in sides:
        count, length = (lax.axis_size(axis), value.shape[dim])
        up = [(i, (i + 1) % count) for i in range(count)]
        down = [(j, i) for i, j in up]
        last = lax.slice_in_dim(value, length - width, length, axis=dim)
        leading = lax.slice_in_dim(value, 0, width, axis=dim)
        before = lax.ppermute(last, axis, up)
        after = lax.ppermute(leading, axis, down)
        value = jnp.concatenate([before, value, after], axis=dim)
    return value


def section_size(substep):
    section_table = jnp.array([1.0 / 3.0, 15.0 / 16.0, 8.0 / 15.0], jnp.float32) * time_step
    selector = (jnp.arange(3, dtype=jnp.int32) == substep[0]).astype(jnp.float32)
    return jnp.sum(section_table * selector)


def local_step(
    padded, amplitudes, patch_ids, axial_speed, radial_diffusion, azimuth_diffusion, step_size
):
    interior = padded[1:-1]
    speed_rows = axial_speed[None, :, None]
    cell_flux = speed_rows * padded + 0.5 * padded * padded
    face_flux = 0.5 * (cell_flux[:-1] + cell_flux[1:]) - 0.5 * dissipation * (
        padded[1:] - padded[:-1]
    )
    axial_term = face_flux[:-1] - face_flux[1:]
    wall_value = jnp.take(amplitudes, patch_ids, axis=0)
    half_turn = interior.shape[2] // 2
    centre_row = jnp.roll(interior[:, :1, :], half_turn, 2)
    stacked = jnp.concatenate([centre_row, interior, wall_value[:, None, :]], axis=1)
    radial = radial_diffusion[None, :, None] * (
        stacked[:, 2:, :] - 2.0 * interior + stacked[:, :-2, :]
    )
    azimuthal = azimuth_diffusion[None, :, None] * (
        jnp.roll(interior, 1, 2) - 2.0 * interior + jnp.roll(interior, -1, 2)
    )
    return interior + step_size * (axial_term + radial + azimuthal)


def gathered_adjoint(
    checkpoint,
    cotangent,
    padded_cot,
    patch_ids,
    patches,
    axial_speed,
    radial_diffusion,
    azimuth_diffusion,
    step_size,
):
    local_slope = axial_speed[None, :, None] + checkpoint
    upper_weight = 0.5 * (local_slope + dissipation)
    lower_weight = 0.5 * (local_slope - dissipation)
    axial_adj = upper_weight * (padded_cot[2:] - cotangent) + lower_weight * (
        cotangent - padded_cot[:-2]
    )
    weighted = radial_diffusion[None, :, None] * cotangent
    half_turn = cotangent.shape[2] // 2
    across = jnp.roll(weighted[:, :1, :], half_turn, 2)
    above_rows = jnp.concatenate([weighted[:, 1:, :], jnp.zeros_like(weighted[:, :1, :])], axis=1)
    below_rows = jnp.concatenate([across, weighted[:, :-1, :]], axis=1)
    radial_adj = above_rows - 2.0 * weighted + below_rows
    azimuthal_adj = azimuth_diffusion[None, :, None] * (
        jnp.roll(cotangent, 1, 2) - 2.0 * cotangent + jnp.roll(cotangent, -1, 2)
    )
    adjoint_state = cotangent + step_size * (axial_adj + radial_adj + azimuthal_adj)
    edge_rows = cotangent[:, -1, :].reshape(-1)
    binned = jax.ops.segment_sum(edge_rows, patch_ids.reshape(-1), num_segments=patches)
    gradient = step_size * radial_diffusion[-1] * binned
    return (adjoint_state, gradient)


def local(
    checkpoint,
    cotangent,
    amplitudes,
    patch_ids,
    substep,
    axial_speed,
    radial_diffusion,
    azimuth_diffusion,
):
    step_size = section_size(substep)
    patches = amplitudes.shape[0]
    padded_state = with_halo(checkpoint, (("ax", 0),), 1)
    padded_cot = with_halo(cotangent, (("ax", 0),), 1)
    advanced = local_step(
        padded_state,
        amplitudes,
        patch_ids,
        axial_speed,
        radial_diffusion,
        azimuth_diffusion,
        step_size,
    )
    adjoint_state, gradient = gathered_adjoint(
        checkpoint,
        cotangent,
        padded_cot,
        patch_ids,
        patches,
        axial_speed,
        radial_diffusion,
        azimuth_diffusion,
        step_size,
    )
    total_cells = checkpoint.shape[0] * lax.axis_size("ax") * checkpoint.shape[2]
    norm_factor = (patches / total_cells) ** 0.5
    summed = lax.psum(gradient, "ax")
    return (advanced, adjoint_state, summed * norm_factor)


def solution(mesh):
    placed = (
        P(("case", "ax"), None, None),
        P(("case", "ax"), None, None),
        P("case"),
        P(("case", "ax"), None),
        P("case"),
        P(),
        P(),
        P(),
    )
    return jax.shard_map(
        local,
        mesh=mesh,
        in_specs=placed,
        out_specs=(P(("case", "ax"), None, None), P(("case", "ax"), None, None), P("case")),
        check_vma=False,
    )
```

profile of v0, /device:TPU:1, one launch (start us, length us, event | category | flops | bytes accessed | tf_op | source)
XLA Modules:
  0.0 154.6 jit_solution(14190793035703883207)
XLA Ops:
  0.6 0.0 copy-start
  0.6 0.1 collective-permute-start.2
  0.8 2.6 %collective-permute-start.3 = (f32[1,384,1536]{2,1,0:T(8,128)}, f32[1,384,1536]{2,1,0:T(8,128)}, u32[]{:S(2)}, u32[]{:S(2)}) collective-permute-start(f32[1,384,1536]{2,1,0:T(8,128)} %param.10), channel_id=1, source_target_pairs={{0,1},{1,2},{2,3},{3,4},{4,5},{5,6},{6,7},{7,8},{8,9},{9,10},{10,1... | collective-permute-start | bytes 7077896 | tf_op jit(solution)/shard_map/ppermute | solution.py:17
  3.4 0.4 collective-permute-start
  3.8 2.4 %collective-permute-start.1 = (f32[1,384,1536]{2,1,0:T(8,128)}, f32[1,384,1536]{2,1,0:T(8,128)}, u32[]{:S(2)}, u32[]{:S(2)}) collective-permute-start(f32[1,384,1536]{2,1,0:T(8,128)} %param.9), channel_id=1, source_target_pairs={{1,0},{2,1},{3,2},{4,3},{5,4},{6,5},{7,6},{8,7},{9,8},{10,9},{11,1... | collective-permute-start | bytes 7077896 | tf_op jit(solution)/shard_map/ppermute | solution.py:18
  6.2 1.9 %broadcast_multiply_fusion = f32[1,384,1536]{2,1,0:T(8,128)S(1)} fusion(f32[1,384,1536]{2,1,0:T(8,128)} %param.10, f32[384]{0:T(512)} %param.15), kind=kLoop, calls=%fused_computation.29 | loop fusion | flops 589824 | bytes 4720128 | tf_op jit(solution)/shard_map/mul | solution.py:69
  8.1 0.0 copy-start.6
  8.1 0.0 copy-start.5
  8.1 2.7 %fusion.23 = (f32[1,383,1536]{2,1,0:T(8,128)}, f32[1,383,1536]{2,1,0:T(8,128)}) fusion(f32[1,384,1536]{2,1,0:T(8,128)S(1)} %broadcast_multiply_fusion), kind=kLoop, calls=%fused_computation.46 | loop fusion | bytes 9412608 | tf_op jit(solution)/shard_map/slice | solution.py:72
  10.7 0.0 copy-done.6
  10.8 0.7 slice.104
  11.4 0.8 slice_reduce_fusion
  12.9 0.0 copy-done.5
  13.0 0.0 copy-done
  13.0 0.0 copy-start.9
  13.0 0.0 copy-start.1
  13.0 9.5 %gather_fusion = f32[1536]{0:T(1024)S(1)} fusion(f32[256]{0:T(256)S(1)} %copy-done, s32[2048]{0:T(1024)S(1)} %pad_clamp_fusion), kind=kCustom, calls=%fused_computation | custom fusion | bytes 18432 | tf_op jit(solution)/shard_map/jit(_take)/gather | solution.py:39
  22.5 0.0 copy-done.9
  22.5 0.6 fusion.18
  24.4 11.1 %scatter_custom_fusion = f32[256]{0:T(256)S(1)} fusion(s32[1536]{0:T(1024)S(1)} %get-tuple-element.3, f32[1536]{0:T(1024)S(1)} %slice_reduce_fusion, f32[]{:T(128)} %constant.12.clone.1), kind=kCustom, calls=%fused_computation.41 | custom fusion | flops 1536 | bytes 1028 | tf_op jit(solution)/shard_map/scatter-add | solution.py:80
  35.5 92.7 %psum.7 = f32[256]{0:T(256)S(1)} all-reduce(f32[256]{0:T(256)S(1)} %broadcast_multiply_fusion.2), channel_id=1, replica_groups=mesh['case'=2,'ax'=16] {'ax'}, use_global_device_ids=true, to_apply=%region_2.3 | all-reduce | flops 256 | bytes 2048 | tf_op jit(solution)/shard_map/psum | solution.py:121
  128.2 1.1 fusion.25
  129.3 0.0 copy-done.1
  129.3 3.3 %fusion.24 = (f32[1,384,1535]{2,1,0:T(8,128)S(1)}, f32[1,384,1535]{2,1,0:T(8,128)S(1)}) fusion(f32[1,384,1536]{2,1,0:T(8,128)} %param.10), kind=kLoop, calls=%fused_computation.47 | loop fusion | bytes 9431040 | tf_op jit(solution)/shard_map/jit(_roll_static)/slice | solution.py:76
  132.6 0.6 broadcast_multiply_fusion.1
  133.2 0.1 fusion.28
  133.3 0.0 copy-start.4
  133.3 0.9 fusion.27
  134.2 0.0 copy-start.2
  134.2 0.0 copy-start.3
  134.2 0.0 copy-start.7
  134.3 0.0 copy-start.8
  134.3 0.0 collective-permute-done
  134.3 2.0 %constant_dynamic-update-slice_fusion.2 = f32[3,384,1536]{2,1,0:T(8,128)S(1)} fusion(f32[1,384,1536]{2,1,0:T(8,128)} %collective-permute-done), kind=kLoop, calls=%fused_computation.35 | loop fusion | bytes 4718592
  136.3 0.0 collective-permute-done.2
  136.3 0.0 collective-permute-done.3
  136.3 0.0 copy-done.4
  136.3 0.5 copy-done.2
  136.8 0.7 copy-done.3
  137.5 0.0 copy-done.7
  137.5 0.0 copy-done.8
  137.5 6.6 %fusion.14 = (f32[1,384,1536]{2,1,0:T(8,128)}, f32[3,384,1536]{2,1,0:T(8,128)S(1)}) fusion(f32[1,384,1536]{2,1,0:T(8,128)S(1)} %copy-done.2, f32[1,383,1536]{2,1,0:T(8,128)S(1)} %copy-done.4, f32[1,1,768]{2,1,0:T(1,128)S(1)} %get-tuple-element.14, f32[1,1,768]{2,1,0:T(1,128)S(1)} %get-tuple-element.13, f32[1,384,1535]{2,1,0:T(8,128)S(1)} %get-tuple-element.10, ...), kind=kLoop, calls=%fused_computation.25 | loop fusion | flops 15335424 | bytes 23998468 | tf_op jit(solution)/shard_map/add | solution.py:78
  144.1 0.0 collective-permute-done.1
  144.1 1.8 %constant_dynamic-update-slice_fusion = f32[3,384,1536]{2,1,0:T(8,128)S(1)} fusion(f32[3,384,1536]{2,1,0:T(8,128)S(1)} %get-tuple-element.6, f32[1,384,1536]{2,1,0:T(8,128)} %collective-permute-done.1), kind=kLoop, calls=%fused_computation.33 | loop fusion | bytes 4718592 | tf_op jit(solution)/shard_map/concatenate | solution.py:19
  145.9 1.1 add_multiply_fusion
  147.0 3.3 %fusion.1 = f32[2,384,1536]{2,1,0:T(8,128)S(1)} fusion(f32[3,384,1536]{2,1,0:T(8,128)S(1)} %add_multiply_fusion, f32[1,384,1536]{2,1,0:T(8,128)} %collective-permute-done.1, f32[1,384,1536]{2,1,0:T(8,128)S(1)} %copy-done.1, f32[1,384,1536]{2,1,0:T(8,128)} %collective-permute-done), kind=kLoop, calls=%fused_computation.5 | loop fusion | flops 7077888 | bytes 21233664 | tf_op jit(solution)/shard_map/sub | solution.py:35
  150.3 4.4 %fusion.7 = f32[1,384,1536]{2,1,0:T(8,128)} fusion(f32[1,384,1536]{2,1,0:T(8,128)S(1)} %copy-done.1, f32[1,1,768]{2,1,0:T(1,128)S(1)} %get-tuple-element.20, f32[1,1,768]{2,1,0:T(1,128)S(1)} %get-tuple-element.19, f32[1,1,1536]{2,1,0:T(1,128)S(1)} %fusion.17, f32[2,384,1536]{2,1,0:T(8,128)S(1)} %fusion.1, f32[1,384,1535]{2,1,0:T(8,128)S(1)} %get-tuple-element.16, ...), kind=kLoop, calls=%fused_computation.13 | loop fusion | flops 10027008 | bytes 14171140 | tf_op jit(solution)/shard_map/add | solution.py:49
  (6 shorter events, 0.1 us)
Async XLA Ops:
  0.6 12.3 %copy-start = (f32[256]{0:T(256)S(1)}, f32[256]{0:T(256)}, u32[]{:S(2)}) copy-start(f32[256]{0:T(256)} %param.11) | copy-start | bytes 3076
  0.6 135.6 %collective-permute-start.2 = (f32[1,384,1536]{2,1,0:T(8,128)}, f32[1,384,1536]{2,1,0:T(8,128)}, u32[]{:S(2)}, u32[]{:S(2)}) collective-permute-start(f32[1,384,1536]{2,1,0:T(8,128)} %param.10), channel_id=1, source_target_pairs={{1,0},{2,1},{3,2},{4,3},{5,4},{6,5},{7,6},{8,7},{9,8},{10,9},{11,1... | collective-permute-start | bytes 7077896 | tf_op jit(solution)/shard_map/ppermute | solution.py:18
  0.8 135.5 %collective-permute-start.3 = (f32[1,384,1536]{2,1,0:T(8,128)}, f32[1,384,1536]{2,1,0:T(8,128)}, u32[]{:S(2)}, u32[]{:S(2)}) collective-permute-start(f32[1,384,1536]{2,1,0:T(8,128)} %param.10), channel_id=1, source_target_pairs={{0,1},{1,2},{2,3},{3,4},{4,5},{5,6},{6,7},{7,8},{8,9},{9,10},{10,1... | collective-permute-start | bytes 7077896 | tf_op jit(solution)/shard_map/ppermute | solution.py:17
  3.4 130.9 %collective-permute-start = (f32[1,384,1536]{2,1,0:T(8,128)}, f32[1,384,1536]{2,1,0:T(8,128)}, u32[]{:S(2)}, u32[]{:S(2)}) collective-permute-start(f32[1,384,1536]{2,1,0:T(8,128)} %param.9), channel_id=1, source_target_pairs={{0,1},{1,2},{2,3},{3,4},{4,5},{5,6},{6,7},{7,8},{8,9},{9,10},{10,1... | collective-permute-start | bytes 7077896 | tf_op jit(solution)/shard_map/ppermute | solution.py:17
  3.8 140.2 %collective-permute-start.1 = (f32[1,384,1536]{2,1,0:T(8,128)}, f32[1,384,1536]{2,1,0:T(8,128)}, u32[]{:S(2)}, u32[]{:S(2)}) collective-permute-start(f32[1,384,1536]{2,1,0:T(8,128)} %param.9), channel_id=1, source_target_pairs={{1,0},{2,1},{3,2},{4,3},{5,4},{6,5},{7,6},{8,7},{9,8},{10,9},{11,1... | collective-permute-start | bytes 7077896 | tf_op jit(solution)/shard_map/ppermute | solution.py:18
  8.1 2.7 %copy-start.6 = (f32[384]{0:T(512)S(1)}, f32[384]{0:T(512)}, u32[]{:S(2)}) copy-start(f32[384]{0:T(512)} %param.15) | copy-start | bytes 4612
  8.1 4.8 %copy-start.5 = (s32[1,1536]{1,0:T(1,128)S(1)}, s32[1,1536]{1,0:T(1,128)}, u32[]{:S(2)}) copy-start(s32[1,1536]{1,0:T(1,128)} %param.12) | copy-start | bytes 18436
  13.0 9.5 %copy-start.9 = (f32[3]{0:T(128)S(1)}, f32[3]{0:T(128)}, u32[]{:S(2)}) copy-start(f32[3]{0:T(128)} %constant.42) | copy-start | bytes 40
  13.0 116.3 %copy-start.1 = (f32[1,384,1536]{2,1,0:T(8,128)S(1)}, f32[1,384,1536]{2,1,0:T(8,128)}, u32[]{:S(2)}) copy-start(f32[1,384,1536]{2,1,0:T(8,128)} %param.9) | copy-start | bytes 7077892
  133.3 3.0 %copy-start.4 = (f32[1,383,1536]{2,1,0:T(8,128)S(1)}, f32[1,383,1536]{2,1,0:T(8,128)}, u32[]{:S(2)}) copy-start(f32[1,383,1536]{2,1,0:T(8,128)} %get-tuple-element.8) | copy-start | bytes 7059460
  134.2 2.6 %copy-start.2 = (f32[1,384,1536]{2,1,0:T(8,128)S(1)}, f32[1,384,1536]{2,1,0:T(8,128)}, u32[]{:S(2)}) copy-start(f32[1,384,1536]{2,1,0:T(8,128)} %param.10) | copy-start | bytes 7077892
  134.2 3.3 %copy-start.3 = (f32[1,383,1536]{2,1,0:T(8,128)S(1)}, f32[1,383,1536]{2,1,0:T(8,128)}, u32[]{:S(2)}) copy-start(f32[1,383,1536]{2,1,0:T(8,128)} %get-tuple-element.7) | copy-start | bytes 7059460
  134.2 3.2 %copy-start.7 = (f32[384]{0:T(512)S(1)}, f32[384]{0:T(512)}, u32[]{:S(2)}) copy-start(f32[384]{0:T(512)} %param.16) | copy-start | bytes 4612
  134.3 3.2 %copy-start.8 = (f32[384]{0:T(512)S(1)}, f32[384]{0:T(512)}, u32[]{:S(2)}) copy-start(f32[384]{0:T(512)} %param.14) | copy-start | bytes 4612
where the time goes:
time: 155 us
  blocking collectives  92.7 us (60%)
  other arithmetic  29.6 us (19%)
  local copies, waits for them, and re-layouts  24.1 us (16%)
  starting transfers between devices  5.53 us (4%)
  between operations  2.81 us (2%)
    psum x1, blocking collectives, local(): summed = lax.psum(gradient, 'ax')  92.7 us
    scatter-add x1, other arithmetic, gathered_adjoint(): jax.ops.segment_sum(edge_rows, patch_ids.reshape(-1), num_segments=patches)  11.1 us
    gather x1, local copies, waits for them, and re-layouts, local_step(): wall_value = jnp.take(amplitudes, patch_ids, axis=0)  9.47 us
    add x1, other arithmetic, gathered_adjoint(): cotangent + step_size * (axial_adj + radial_adj + azimuthal_adj)  6.56 us
    slice x2, local copies, waits for them, and re-layouts, gathered_adjoint(): jnp.roll(cotangent, -1, 2)  4.4 us
    add x1, other arithmetic, local_step(): return interior + step_size * (axial_term + radial + azimuthal)  4.36 us
    sub x1, other arithmetic, local_step(): 0.5 * (cell_flux[:-1] + cell_flux[1:])  3.26 us
    unnamed x21, local copies, waits for them, and re-layouts  3.24 us
  transfers between devices with their start and end apart: 4, of which 0 were waited for; matrix products, arithmetic and copies ran while one was open for 27% of the time, Pallas kernels for 0%

commit v1 on v0

v1 whole, which is shorter than its diff:
```python
import functools

import jax
import jax.numpy as jnp
from jax import lax
from jax.experimental import pallas as pl
from jax.experimental.pallas import tpu as pltpu
from jax.sharding import PartitionSpec as P

time_step = 0.6
dissipation = 2.0

STATE_CHUNKS = 1
COT_CHUNKS = 4
BLOCK_ROWS = 48


def section_size(substep):
    section_table = jnp.array([1.0 / 3.0, 15.0 / 16.0, 8.0 / 15.0], jnp.float32) * time_step
    selector = (jnp.arange(3, dtype=jnp.int32) == substep[0]).astype(jnp.float32)
    return jnp.sum(section_table * selector)


def on_pairs(count):
    return [(i, i ^ 1) for i in range(count)]


def off_pairs(count):
    return [(i, (i + 1) % count if i % 2 else (i - 1) % count) for i in range(count)]


def all_sum(value, axis):
    count = lax.axis_size(axis)
    if count & (count - 1):
        return lax.psum(value, axis)
    step = 1
    while step < count:
        value = value + lax.ppermute(value, axis, [(i, i ^ step) for i in range(count)])
        step *= 2
    return value


def state_update(scal, base, near, far, speed, out):
    step, side = scal[0], scal[1]
    u = speed[...]
    a, b = near[0], far[0]
    flux = b * (u + 0.5 * b) - a * (u + 0.5 * a)
    out[0] = base[0] + step * (a + b + (0.5 * side) * flux)


def cot_update(scal, base, near, far, state, speed, out):
    step, side = scal[0], scal[1]
    a, b = near[0], far[0]
    slope = (0.5 * side) * (speed[...] + state[0])
    out[0] = base[0] + step * (a + b + slope * (a - b))


def chunk_update(body, scal, base, whole, part, speed, start, rows):
    width = base.shape[2]
    block = min(BLOCK_ROWS, rows)
    first = start // block
    full = pl.BlockSpec((1, block, width), lambda i: (0, first + i, 0))
    piece = pl.BlockSpec((1, block, width), lambda i: (0, i, 0))
    column = pl.BlockSpec((block, 1), lambda i: (first + i, 0))
    return pl.pallas_call(
        body,
        grid=(rows // block,),
        out_shape=jax.ShapeDtypeStruct(base.shape, base.dtype),
        in_specs=[pl.BlockSpec(memory_space=pltpu.SMEM), full]
        + [piece] * len(part)
        + [full] * len(whole)
        + [column],
        out_specs=full,
        input_output_aliases={1: 0},
        cost_estimate=pl.CostEstimate(
            flops=10 * rows * width, bytes_accessed=4 * rows * width * 5, transcendentals=0
        ),
    )(scal, base, *part, *whole, speed)


def local_parts(
    checkpoint, cotangent, amplitudes, patch_ids, radial_diffusion, azimuth_diffusion, step_size
):
    half_turn = checkpoint.shape[2] // 2
    rd = radial_diffusion[None, :, None]
    ad = azimuth_diffusion[None, :, None]
    wall_value = jnp.take(amplitudes, patch_ids, axis=0)
    centre_row = jnp.roll(checkpoint[:, :1, :], half_turn, 2)
    stacked = jnp.concatenate([centre_row, checkpoint, wall_value[:, None, :]], axis=1)
    radial = rd * (stacked[:, 2:, :] - 2.0 * checkpoint + stacked[:, :-2, :])
    azimuthal = ad * (jnp.roll(checkpoint, 1, 2) - 2.0 * checkpoint + jnp.roll(checkpoint, -1, 2))
    state_base = checkpoint + step_size * (radial + azimuthal - dissipation * checkpoint)

    weighted = rd * cotangent
    across = jnp.roll(weighted[:, :1, :], half_turn, 2)
    above = jnp.concatenate([weighted[:, 1:, :], jnp.zeros_like(weighted[:, :1, :])], axis=1)
    below = jnp.concatenate([across, weighted[:, :-1, :]], axis=1)
    radial_adj = above - 2.0 * weighted + below
    azimuthal_adj = ad * (
        jnp.roll(cotangent, 1, 2) - 2.0 * cotangent + jnp.roll(cotangent, -1, 2)
    )
    cot_base = cotangent + step_size * (radial_adj + azimuthal_adj - dissipation * cotangent)
    return state_base, cot_base


def local(
    checkpoint,
    cotangent,
    amplitudes,
    patch_ids,
    substep,
    axial_speed,
    radial_diffusion,
    azimuth_diffusion,
):
    count = lax.axis_size("ax")
    rows = checkpoint.shape[1]
    near, far = on_pairs(count), off_pairs(count)

    def exchange(value, pieces):
        size = rows // pieces
        return [
            (
                lax.ppermute(value[:, n * size : (n + 1) * size], "ax", far),
                lax.ppermute(value[:, n * size : (n + 1) * size], "ax", near),
            )
            for n in range(pieces)
        ]

    state_halo = exchange(checkpoint, STATE_CHUNKS)
    cot_halo = exchange(cotangent, COT_CHUNKS)

    step_size = section_size(substep)
    patches = amplitudes.shape[0]
    side = 1.0 - 2.0 * (lax.axis_index("ax") % 2).astype(jnp.float32)
    scal = jnp.stack([step_size, side])
    speed = axial_speed[:, None]

    edge_rows = cotangent[:, -1, :].reshape(-1)
    binned = jax.ops.segment_sum(edge_rows, patch_ids.reshape(-1), num_segments=patches)
    total_cells = checkpoint.shape[0] * count * checkpoint.shape[2]
    norm_factor = (patches / total_cells) ** 0.5
    gradient = all_sum(step_size * radial_diffusion[-1] * binned, "ax") * norm_factor

    advanced, adjoint = local_parts(
        checkpoint, cotangent, amplitudes, patch_ids, radial_diffusion, azimuth_diffusion, step_size
    )
    size = rows // STATE_CHUNKS
    for n, (b, a) in enumerate(state_halo):
        advanced = chunk_update(state_update, scal, advanced, [], [a, b], speed, n * size, size)
    size = rows // COT_CHUNKS
    for n, (b, a) in enumerate(cot_halo):
        adjoint = chunk_update(
            cot_update, scal, adjoint, [checkpoint], [a, b], speed, n * size, size
        )
    return (advanced, adjoint, gradient)


def solution(mesh):
    placed = (
        P(("case", "ax"), None, None),
        P(("case", "ax"), None, None),
        P("case"),
        P(("case", "ax"), None),
        P("case"),
        P(),
        P(),
        P(),
    )
    return jax.shard_map(
        local,
        mesh=mesh,
        in_specs=placed,
        out_specs=(P(("case", "ax"), None, None), P(("case", "ax"), None, None), P("case")),
        check_vma=False,
    )
```

time: 155 us -> 132 us (0.85)
  blocking collectives: 92.7 us -> 0 us
  waiting for transfers between devices: 0.01 us -> 48.4 us
  Pallas kernels: 0 us -> 17.6 us
  starting transfers between devices: 5.53 us -> 19.1 us
  other arithmetic: 29.6 us -> 23.9 us
  local copies, waits for them, and re-layouts: 24.1 us -> 19.5 us
    psum x1 -> x0, blocking collectives: 92.7 us -> none  [local(): summed = lax.psum(gradient, 'ax')]
    ppermute x4 -> x14, waiting for transfers between devices: 0.01 us -> 48.4 us  [the longest x4 25.6 us: all_sum(): lax.ppermute(value, axis, [(i, i ^ step) for i in range(count)])]
    pallas_call x0 -> x5, Pallas kernels: none -> 17.6 us  [chunk_update(): pl.pallas_call(body, grid=(rows // block,), out_shape=jax.ShapeDtypeStruc...]
    ppermute x4 -> x14, starting transfers between devices: 5.53 us -> 19.1 us  [the longest x5 10.7 us: exchange(): lax.ppermute(value[:, n * size:(n + 1) * size], 'ax', near)]
    add x3 -> x4, other arithmetic: 12.1 us -> 3.93 us  [the longest x1 3.92 us: local_parts(): cotangent + step_size * (radial_adj + azimuthal_adj - dissipation * cotan...]
    mul x3, other arithmetic: 2.46 us -> 7.01 us  [the longest x1 6.44 us: local_parts(): weighted = rd * cotangent]
    sub x1 -> x0, other arithmetic: 3.26 us -> none  [local_step(): 0.5 * (cell_flux[:-1] + cell_flux[1:])]
    unnamed x21 -> x24, local copies, waits for them, and re-layouts: 3.24 us -> 0.06 us
  transfers between devices with their start and end apart: 4 -> 14, of which waited for: 0 -> 6; matrix products, arithmetic and copies ran while one was open for 27% -> 31% of each run, Pallas kernels for 0% -> 8%
where the time goes in v1:
time: 132 us; the launch traced here: 131 us
  waiting for transfers between devices  48.4 us (37%)
  other arithmetic  23.9 us (18%)
  local copies, waits for them, and re-layouts  19.5 us (15%)
  starting transfers between devices  19.1 us (14%)
  Pallas kernels  17.6 us (13%)
  between operations  2.75 us (2%)
    ppermute x4, waiting for transfers between devices, all_sum(): lax.ppermute(value, axis, [(i, i ^ step) for i in range(count)])  25.6 us
    ppermute x5, waiting for transfers between devices, exchange(): lax.ppermute(value[:, n * size:(n + 1) * size], 'ax', far)  22.8 us
    pallas_call x5, Pallas kernels, chunk_update(): pl.pallas_call(body, grid=(rows // block,), out_shape=jax.ShapeDtypeStruc...  17.6 us
    scatter-add x1, other arithmetic, local(): jax.ops.segment_sum(edge_rows, patch_ids.reshape(-1), num_segments=patches)  11.1 us
    ppermute x5, starting transfers between devices, exchange(): lax.ppermute(value[:, n * size:(n + 1) * size], 'ax', near)  10.7 us
    gather x1, local copies, waits for them, and re-layouts, local_parts(): wall_value = jnp.take(amplitudes, patch_ids, axis=0)  9.47 us
    mul x1, other arithmetic, local_parts(): weighted = rd * cotangent  6.44 us
    ppermute x4, starting transfers between devices, all_sum(): lax.ppermute(value, axis, [(i, i ^ step) for i in range(count)])  5.59 us
  transfers between devices with their start and end apart: 14, of which 6 were waited for; matrix products, arithmetic and copies ran while one was open for 31% of the time, Pallas kernels for 8%

profile of v1, /device:TPU:1, one launch (start us, length us, event | category | flops | bytes accessed | tf_op | source)
XLA Modules:
  0.0 131.1 jit_solution(14438302475931153365)
XLA Ops:
  0.6 0.0 copy-start
  0.6 0.0 copy-start.11
  0.7 0.0 copy-start.1
  0.7 3.0 %fusion.21 = (f32[1,96,1536]{2,1,0:T(8,128)S(1)}, f32[1,96,1536]{2,1,0:T(8,128)}, f32[1,96,1536]{2,1,0:T(8,128)}, f32[1,96,1536]{2,1,0:T(8,128)}) fusion(f32[1,384,1536]{2,1,0:T(8,128)} %param.10), kind=kLoop, calls=%fused_computation.38 | loop fusion | bytes 4718592 | tf_op jit(solution)/shard_map/slice | solution.py:125
  3.7 0.1 collective-permute-start.2
  3.8 2.5 %collective-permute-start.3 = (f32[1,96,1536]{2,1,0:T(8,128)}, f32[1,96,1536]{2,1,0:T(8,128)}, u32[]{:S(2)}, u32[]{:S(2)}) collective-permute-start(f32[1,96,1536]{2,1,0:T(8,128)} %get-tuple-element.7), channel_id=1, source_target_pairs={{0,15},{1,2},{2,1},{3,4},{4,3},{5,6},{6,5},{7,8},{8,7},{9,10},{10,... | collective-permute-start | bytes 1769480 | tf_op jit(solution)/shard_map/ppermute | solution.py:124
  6.3 3.5 %collective-permute-start = (f32[1,384,1536]{2,1,0:T(8,128)S(1)}, f32[1,384,1536]{2,1,0:T(8,128)}, u32[]{:S(2)}, u32[]{:S(2)}) collective-permute-start(f32[1,384,1536]{2,1,0:T(8,128)S(1)} %copy-done.1), channel_id=1, source_target_pairs={{0,1},{1,0},{2,3},{3,2},{4,5},{5,4},{6,7},{7,6},{8,9},{9,8},{10,11... | collective-permute-start | bytes 7077896 | tf_op jit(solution)/shard_map/ppermute | solution.py:125
  9.9 0.0 collective-permute-start.1
  9.9 0.8 slice_reduce_fusion
  11.4 0.6 slice.104
  12.0 0.6 fusion.16
  13.8 11.1 %scatter_custom_fusion = f32[256]{0:T(256)S(1)} fusion(s32[1536]{0:T(1024)S(1)} %get-tuple-element.3, f32[1536]{0:T(1024)S(1)} %slice_reduce_fusion, f32[]{:T(128)} %constant.19.clone.1), kind=kCustom, calls=%fused_computation.33 | custom fusion | flops 1536 | bytes 1028 | tf_op jit(solution)/shard_map/scatter-add | solution.py:140
  24.9 0.7 collective-permute-start.10
  25.7 3.1 %fusion.26 = (f32[1,384,1535]{2,1,0:T(8,128)}, f32[1,384,1535]{2,1,0:T(8,128)}) fusion(f32[1,384,1536]{2,1,0:T(8,128)S(1)} %copy-done.1), kind=kLoop, calls=%fused_computation.43 | loop fusion | bytes 9431040 | tf_op jit(solution)/shard_map/jit(_roll_static)/slice | solution.py:91
  28.8 0.1 fusion.27
  28.9 0.0 copy-start.9
  28.9 9.5 %gather_fusion = f32[1536]{0:T(1024)S(1)} fusion(f32[256]{0:T(256)S(1)} %copy-done, s32[2048]{0:T(1024)S(1)} %pad_clamp_fusion), kind=kCustom, calls=%fused_computation | custom fusion | bytes 18432 | tf_op jit(solution)/shard_map/jit(_take)/gather | solution.py:87
  38.5 6.4 %broadcast_multiply_fusion = (f32[1,384,1536]{2,1,0:T(8,128)S(1)}, f32[1,384,1536]{2,1,0:T(8,128)}) fusion(f32[1,384,1536]{2,1,0:T(8,128)} %param.10, f32[384]{0:T(512)S(1)} %copy-done.8, f32[1,384,1536]{2,1,0:T(8,128)S(1)} %copy-done.1, f32[1,384,1]{2,1,0:T(8,128)S(1)} %get-tuple-element.19, f32[1,384,1535]{2,1,0:T(8,128)} %get-tuple-element.17, ...), kind=kLoop, calls=%fused_computation.23 | loop fusion | flops 10027008 | bytes 14171140 | tf_op jit(solution)/shard_map/mul | solution.py:94
  44.9 0.0 collective-permute-done.10
  44.9 1.3 collective-permute-start.11
  46.2 0.5 fusion.22
  46.7 23.6 %collective-permute-done.11 = f32[256]{0:T(256)S(1)} collective-permute-done((f32[256]{0:T(256)S(1)}, f32[256]{0:T(256)S(1)}, u32[]{:S(2)}, u32[]{:S(2)}) %collective-permute-start.11) | collective-permute-done | bytes 1056 | tf_op jit(solution)/shard_map/ppermute | solution.py:38
  70.3 1.3 collective-permute-start.12
  71.6 0.1 fusion.24
  71.7 1.0 collective-permute-done.12
  72.7 2.3 %collective-permute-start.13 = (f32[256]{0:T(256)S(1)}, f32[256]{0:T(256)S(1)}, u32[]{:S(2)}, u32[]{:S(2)}) collective-permute-start(f32[256]{0:T(256)S(1)} %add.65), channel_id=1, source_target_pairs={{0,8},{1,9},{2,10},{3,11},{4,12},{5,13},{6,14},{7,15},{8,0},{9,1},... | collective-permute-start | bytes 3080 | tf_op jit(solution)/shard_map/ppermute | solution.py:38
  75.0 1.0 collective-permute-done.13
  76.0 4.0 %collective-permute-start.4 = (f32[1,96,1536]{2,1,0:T(8,128)S(1)}, f32[1,96,1536]{2,1,0:T(8,128)S(1)}, u32[]{:S(2)}, u32[]{:S(2)}) collective-permute-start(f32[1,96,1536]{2,1,0:T(8,128)S(1)} %copy-done.3), channel_id=1, source_target_pairs={{0,1},{1,0},{2,3},{3,2},{4,5},{5,4},{6,7},{7,6},{8,9},{9,8},{10,11... | collective-permute-start | bytes 1769480 | tf_op jit(solution)/shard_map/ppermute | solution.py:125
  80.0 0.0 collective-permute-done.2.near
  80.0 0.0 collective-permute-start.5
  80.0 0.0 collective-permute-done.3.far
  80.0 3.0 %collective-permute-start.6 = (f32[1,96,1536]{2,1,0:T(8,128)}, f32[1,96,1536]{2,1,0:T(8,128)S(1)}, u32[]{:S(2)}, u32[]{:S(2)}) collective-permute-start(f32[1,96,1536]{2,1,0:T(8,128)} %get-tuple-element.8), channel_id=1, source_target_pairs={{0,1},{1,0},{2,3},{3,2},{4,5},{5,4},{6,7},{7,6},{8,9},{9,8},{10,11... | collective-permute-start | bytes 1769480 | tf_op jit(solution)/shard_map/ppermute | solution.py:125
  83.1 0.9 fusion.23
  84.0 0.2 collective-permute-start.7
  84.2 17.8 %collective-permute-done.5.far = f32[1,96,1536]{2,1,0:T(8,128)S(1)} collective-permute-done((f32[1,96,1536]{2,1,0:T(8,128)S(1)}, f32[1,96,1536]{2,1,0:T(8,128)S(1)}, u32[]{:S(2)}, u32[]{:S(2)}) %collective-permute-start.5) | collective-permute-done | bytes 589856 | tf_op jit(solution)/shard_map/ppermute | solution.py:124
  102.0 0.1 collective-permute-start.9
  102.1 0.0 copy-start.10
  102.1 3.9 %fusion.12.base = f32[1,384,1536]{2,1,0:T(8,128)} fusion(f32[1,384,1536]{2,1,0:T(8,128)S(1)} %copy-done.2, f32[1,383,1536]{2,1,0:T(8,128)S(1)} %get-tuple-element.10, f32[1,1,768]{2,1,0:T(1,128)S(1)} %get-tuple-element.16, f32[1,1,768]{2,1,0:T(1,128)S(1)} %get-tuple-element.15, f32[1,384,1535]{2,1,0:T(8,128)S(1)} %get-tuple-element.12, ...), kind=kLoop, calls=%fused_computation.19 | loop fusion | flops 9437184 | bytes 14152708 | tf_op jit(solution)/shard_map/add | solution.py:102
  106.1 0.8 broadcast_in_dim.25.speed
  106.8 1.1 pad_maximum_fusion.3.scal
  108.0 0.6 add_multiply_fusion
  108.6 2.5 %shard_map.113.base = f32[1,384,1536]{2,1,0:T(8,128)} custom-call(f32[2]{0:T(128)} %pad_maximum_fusion.3.scal, f32[1,384,1536]{2,1,0:T(8,128)} %fusion.12.base, f32[1,96,1536]{2,1,0:T(8,128)} %collective-permute-done.2.near, f32[1,96,1536]{2,1,0:T(8,128)} %collective-permute-done.3.far, f32[1,384,1536]{2,1,0:T(8,128)} %state.7, ...), custom_call_target="tpu_custom_call", output_to_operand_aliasing={{}: (1, {})} | custom-call | flops 1474560 | bytes 2949120 | tf_op jit(solution)/shard_map/pallas_call | solution.py:65
  111.1 2.5 %shard_map.114.base = f32[1,384,1536]{2,1,0:T(8,128)} custom-call(f32[2]{0:T(128)} %pad_maximum_fusion.3.scal, f32[1,384,1536]{2,1,0:T(8,128)} %shard_map.113.base, f32[1,96,1536]{2,1,0:T(8,128)} %copy-done.4, f32[1,96,1536]{2,1,0:T(8,128)} %copy-done.5, f32[1,384,1536]{2,1,0:T(8,128)} %state.7, ...), custom_call_target="tpu_custom_call", output_to_operand_aliasing={{}: (1, {})} | custom-call | flops 1474560 | bytes 2949120 | tf_op jit(solution)/shard_map/pallas_call | solution.py:65
  113.6 1.1 collective-permute-done.7.far
  114.7 2.5 %shard_map.115.base = f32[1,384,1536]{2,1,0:T(8,128)} custom-call(f32[2]{0:T(128)} %pad_maximum_fusion.3.scal, f32[1,384,1536]{2,1,0:T(8,128)} %shard_map.114.base, f32[1,96,1536]{2,1,0:T(8,128)} %copy-done.6, f32[1,96,1536]{2,1,0:T(8,128)} %collective-permute-done.7.far, f32[1,384,1536]{2,1,0:T(8,128)} %state.7, ...), custom_call_target="tpu_custom_call", output_to_operand_aliasing={{}: (1, {})} | custom-call | flops 1474560 | bytes 2949120 | tf_op jit(solution)/shard_map/pallas_call | solution.py:65
  117.3 3.8 %collective-permute-done.9.far = f32[1,96,1536]{2,1,0:T(8,128)} collective-permute-done((f32[1,96,1536]{2,1,0:T(8,128)S(1)}, f32[1,96,1536]{2,1,0:T(8,128)}, u32[]{:S(2)}, u32[]{:S(2)}) %collective-permute-start.9) | collective-permute-done | bytes 589856 | tf_op jit(solution)/shard_map/ppermute | solution.py:124
  121.1 2.5 %shard_map.116 = f32[1,384,1536]{2,1,0:T(8,128)} custom-call(f32[2]{0:T(128)} %pad_maximum_fusion.3.scal, f32[1,384,1536]{2,1,0:T(8,128)} %shard_map.115.base, f32[1,96,1536]{2,1,0:T(8,128)} %collective-permute-done.8.near, f32[1,96,1536]{2,1,0:T(8,128)} %collective-permute-done.9.far, f32[1,384,1536]{2,1,0:T(8,128)} %state.7, ...), custom_call_target="tpu_custom_call", output_to_operand_aliasing={{}: (1, {})} | custom-call | flops 1474560 | bytes 2949120 | tf_op jit(solution)/shard_map/pallas_call | solution.py:65
  123.6 7.5 %shard_map.112 = f32[1,384,1536]{2,1,0:T(8,128)} custom-call(f32[2]{0:T(128)} %pad_maximum_fusion.3.scal, f32[1,384,1536]{2,1,0:T(8,128)} %get-tuple-element.24.base, f32[1,384,1536]{2,1,0:T(8,128)} %collective-permute-done.near, f32[1,384,1536]{2,1,0:T(8,128)} %collective-permute-done.1.far, ...), custom_call_target="tpu_custom_call", output_to_operand_aliasing={{}: (1, {})} | custom-call | flops 5898240 | bytes 11796480 | tf_op jit(solution)/shard_map/pallas_call | solution.py:65
  (34 shorter events, 0.1 us)
Async XLA Ops:
  0.6 28.3 %copy-start = (f32[256]{0:T(256)S(1)}, f32[256]{0:T(256)}, u32[]{:S(2)}) copy-start(f32[256]{0:T(256)} %param.11) | copy-start | bytes 3076
  0.6 11.3 %copy-start.11 = (f32[3]{0:T(128)S(1)}, f32[3]{0:T(128)}, u32[]{:S(2)}) copy-start(f32[3]{0:T(128)} %constant.55) | copy-start | bytes 40
  0.7 5.7 %copy-start.1 = (f32[1,384,1536]{2,1,0:T(8,128)S(1)}, f32[1,384,1536]{2,1,0:T(8,128)}, u32[]{:S(2)}) copy-start(f32[1,384,1536]{2,1,0:T(8,128)} %state.7) | copy-start | bytes 7077892
  0.7 10.7 %copy-start.7 = (s32[1,1536]{1,0:T(1,128)S(1)}, s32[1,1536]{1,0:T(1,128)}, u32[]{:S(2)}) copy-start(s32[1,1536]{1,0:T(1,128)} %param.12) | copy-start | bytes 18436
  0.7 10.7 %copy-start.8 = (f32[384]{0:T(512)S(1)}, f32[384]{0:T(512)}, u32[]{:S(2)}) copy-start(f32[384]{0:T(512)} %param.15) | copy-start | bytes 4612
  3.7 76.3 %collective-permute-start.2 = (f32[1,96,1536]{2,1,0:T(8,128)}, f32[1,96,1536]{2,1,0:T(8,128)}, u32[]{:S(2)}, u32[]{:S(2)}) collective-permute-start(f32[1,96,1536]{2,1,0:T(8,128)} %get-tuple-element.7), channel_id=1, source_target_pairs={{0,1},{1,0},{2,3},{3,2},{4,5},{5,4},{6,7},{7,6},{8,9},{9,8},{10,11... | collective-permute-start | bytes 1769480 | tf_op jit(solution)/shard_map/ppermute | solution.py:125
  3.8 76.3 %collective-permute-start.3 = (f32[1,96,1536]{2,1,0:T(8,128)}, f32[1,96,1536]{2,1,0:T(8,128)}, u32[]{:S(2)}, u32[]{:S(2)}) collective-permute-start(f32[1,96,1536]{2,1,0:T(8,128)} %get-tuple-element.7), channel_id=1, source_target_pairs={{0,15},{1,2},{2,1},{3,4},{4,3},{5,6},{6,5},{7,8},{8,7},{9,10},{10,... | collective-permute-start | bytes 1769480 | tf_op jit(solution)/shard_map/ppermute | solution.py:124
  6.3 117.3 %collective-permute-start = (f32[1,384,1536]{2,1,0:T(8,128)S(1)}, f32[1,384,1536]{2,1,0:T(8,128)}, u32[]{:S(2)}, u32[]{:S(2)}) collective-permute-start(f32[1,384,1536]{2,1,0:T(8,128)S(1)} %copy-done.1), channel_id=1, source_target_pairs={{0,1},{1,0},{2,3},{3,2},{4,5},{5,4},{6,7},{7,6},{8,9},{9,8},{10,11... | collective-permute-start | bytes 7077896 | tf_op jit(solution)/shard_map/ppermute | solution.py:125
  9.9 113.7 %collective-permute-start.1 = (f32[1,384,1536]{2,1,0:T(8,128)S(1)}, f32[1,384,1536]{2,1,0:T(8,128)}, u32[]{:S(2)}, u32[]{:S(2)}) collective-permute-start(f32[1,384,1536]{2,1,0:T(8,128)S(1)} %copy-done.1), channel_id=1, source_target_pairs={{0,15},{1,2},{2,1},{3,4},{4,3},{5,6},{6,5},{7,8},{8,7},{9,10},{10,... | collective-permute-start | bytes 7077896 | tf_op jit(solution)/shard_map/ppermute | solution.py:124
  24.9 19.9 %collective-permute-start.10 = (f32[256]{0:T(256)S(1)}, f32[256]{0:T(256)S(1)}, u32[]{:S(2)}, u32[]{:S(2)}) collective-permute-start(f32[256]{0:T(256)S(1)} %broadcast_multiply_fusion.1), channel_id=1, source_target_pairs={{0,1},{1,0},{2,3},{3,2},{4,5},{5,4},{6,7},{7,6},{8,9},{9,8},{10,11... | collective-permute-start | bytes 3080 | tf_op jit(solution)/shard_map/ppermute | solution.py:38
  28.9 9.5 %copy-start.9 = (f32[384]{0:T(512)S(1)}, f32[384]{0:T(512)}, u32[]{:S(2)}) copy-start(f32[384]{0:T(512)} %param.16) | copy-start | bytes 4612
  44.9 25.4 %collective-permute-start.11 = (f32[256]{0:T(256)S(1)}, f32[256]{0:T(256)S(1)}, u32[]{:S(2)}, u32[]{:S(2)}) collective-permute-start(f32[256]{0:T(256)S(1)} %fusion.29), channel_id=1, source_target_pairs={{0,2},{1,3},{2,0},{3,1},{4,6},{5,7},{6,4},{7,5},{8,10},{9,11},{10,... | collective-permute-start | bytes 3080 | tf_op jit(solution)/shard_map/ppermute | solution.py:38
  46.2 25.4 %copy-start.2 = (f32[1,384,1536]{2,1,0:T(8,128)S(1)}, f32[1,384,1536]{2,1,0:T(8,128)}, u32[]{:S(2)}) copy-start(f32[1,384,1536]{2,1,0:T(8,128)} %param.10) | copy-start | bytes 7077892
  46.2 29.8 %copy-start.3 = (f32[1,96,1536]{2,1,0:T(8,128)S(1)}, f32[1,96,1536]{2,1,0:T(8,128)}, u32[]{:S(2)}) copy-start(f32[1,96,1536]{2,1,0:T(8,128)} %get-tuple-element.6) | copy-start | bytes 1769476
  70.3 2.4 %collective-permute-start.12 = (f32[256]{0:T(256)S(1)}, f32[256]{0:T(256)S(1)}, u32[]{:S(2)}, u32[]{:S(2)}) collective-permute-start(f32[256]{0:T(256)S(1)} %add.64), channel_id=1, source_target_pairs={{0,4},{1,5},{2,6},{3,7},{4,0},{5,1},{6,2},{7,3},{8,12},{9,13},{10,... | collective-permute-start | bytes 3080 | tf_op jit(solution)/shard_map/ppermute | solution.py:38
  72.7 3.3 %collective-permute-start.13 = (f32[256]{0:T(256)S(1)}, f32[256]{0:T(256)S(1)}, u32[]{:S(2)}, u32[]{:S(2)}) collective-permute-start(f32[256]{0:T(256)S(1)} %add.65), channel_id=1, source_target_pairs={{0,8},{1,9},{2,10},{3,11},{4,12},{5,13},{6,14},{7,15},{8,0},{9,1},... | collective-permute-start | bytes 3080 | tf_op jit(solution)/shard_map/ppermute | solution.py:38
  76.0 8.0 %collective-permute-start.4 = (f32[1,96,1536]{2,1,0:T(8,128)S(1)}, f32[1,96,1536]{2,1,0:T(8,128)S(1)}, u32[]{:S(2)}, u32[]{:S(2)}) collective-permute-start(f32[1,96,1536]{2,1,0:T(8,128)S(1)} %copy-done.3), channel_id=1, source_target_pairs={{0,1},{1,0},{2,3},{3,2},{4,5},{5,4},{6,7},{7,6},{8,9},{9,8},{10,11... | collective-permute-start | bytes 1769480 | tf_op jit(solution)/shard_map/ppermute | solution.py:125
  80.0 21.9 %collective-permute-start.5 = (f32[1,96,1536]{2,1,0:T(8,128)S(1)}, f32[1,96,1536]{2,1,0:T(8,128)S(1)}, u32[]{:S(2)}, u32[]{:S(2)}) collective-permute-start(f32[1,96,1536]{2,1,0:T(8,128)S(1)} %copy-done.3), channel_id=1, source_target_pairs={{0,15},{1,2},{2,1},{3,4},{4,3},{5,6},{6,5},{7,8},{8,7},{9,10},{10,... | collective-permute-start | bytes 1769480 | tf_op jit(solution)/shard_map/ppermute | solution.py:124
  80.0 21.9 %collective-permute-start.6 = (f32[1,96,1536]{2,1,0:T(8,128)}, f32[1,96,1536]{2,1,0:T(8,128)S(1)}, u32[]{:S(2)}, u32[]{:S(2)}) collective-permute-start(f32[1,96,1536]{2,1,0:T(8,128)} %get-tuple-element.8), channel_id=1, source_target_pairs={{0,1},{1,0},{2,3},{3,2},{4,5},{5,4},{6,7},{7,6},{8,9},{9,8},{10,11... | collective-permute-start | bytes 1769480 | tf_op jit(solution)/shard_map/ppermute | solution.py:125
  84.0 22.0 %copy-start.4 = (f32[1,96,1536]{2,1,0:T(8,128)}, f32[1,96,1536]{2,1,0:T(8,128)S(1)}, u32[]{:S(2)}) copy-start(f32[1,96,1536]{2,1,0:T(8,128)S(1)} %collective-permute-done.4.near) | copy-start | bytes 1769476
  84.0 30.7 %collective-permute-start.7 = (f32[1,96,1536]{2,1,0:T(8,128)}, f32[1,96,1536]{2,1,0:T(8,128)}, u32[]{:S(2)}, u32[]{:S(2)}) collective-permute-start(f32[1,96,1536]{2,1,0:T(8,128)} %get-tuple-element.8), channel_id=1, source_target_pairs={{0,15},{1,2},{2,1},{3,4},{4,3},{5,6},{6,5},{7,8},{8,7},{9,10},{10,... | collective-permute-start | bytes 1769480 | tf_op jit(solution)/shard_map/ppermute | solution.py:124
  102.0 4.0 %copy-start.5 = (f32[1,96,1536]{2,1,0:T(8,128)}, f32[1,96,1536]{2,1,0:T(8,128)S(1)}, u32[]{:S(2)}) copy-start(f32[1,96,1536]{2,1,0:T(8,128)S(1)} %collective-permute-done.5.far) | copy-start | bytes 1769476
  102.0 15.3 %collective-permute-start.8 = (f32[1,96,1536]{2,1,0:T(8,128)S(1)}, f32[1,96,1536]{2,1,0:T(8,128)}, u32[]{:S(2)}, u32[]{:S(2)}) collective-permute-start(f32[1,96,1536]{2,1,0:T(8,128)S(1)} %get-tuple-element.5), channel_id=1, source_target_pairs={{0,1},{1,0},{2,3},{3,2},{4,5},{5,4},{6,7},{7,6},{8,9},{9,8},{10,11... | collective-permute-start | bytes 1769480 | tf_op jit(solution)/shard_map/ppermute | solution.py:125
  102.0 4.0 %copy-start.6 = (f32[1,96,1536]{2,1,0:T(8,128)}, f32[1,96,1536]{2,1,0:T(8,128)S(1)}, u32[]{:S(2)}) copy-start(f32[1,96,1536]{2,1,0:T(8,128)S(1)} %collective-permute-done.6.near) | copy-start | bytes 1769476
  102.0 19.0 %collective-permute-start.9 = (f32[1,96,1536]{2,1,0:T(8,128)S(1)}, f32[1,96,1536]{2,1,0:T(8,128)}, u32[]{:S(2)}, u32[]{:S(2)}) collective-permute-start(f32[1,96,1536]{2,1,0:T(8,128)S(1)} %get-tuple-element.5), channel_id=1, source_target_pairs={{0,15},{1,2},{2,1},{3,4},{4,3},{5,6},{6,5},{7,8},{8,7},{9,10},{10,... | collective-permute-start | bytes 1769480 | tf_op jit(solution)/shard_map/ppermute | solution.py:124
  102.1 4.0 %copy-start.10 = (f32[384]{0:T(512)S(1)}, f32[384]{0:T(512)}, u32[]{:S(2)}) copy-start(f32[384]{0:T(512)} %param.14) | copy-start | bytes 4612

commit v2 on v1

--- a/solution.py
+++ b/solution.py
@@ -1,4 +1,4 @@
-import functools
+import math
 
 import jax
 import jax.numpy as jnp
@@ -10,8 +10,8 @@
 time_step = 0.6
 dissipation = 2.0
 
-STATE_CHUNKS = 1
-COT_CHUNKS = 4
+STATE_PARTS = 4
+STATE_CUTS = (0, 3, 4)
 BLOCK_ROWS = 48
 
 
@@ -29,35 +29,31 @@
     return [(i, (i + 1) % count if i % 2 else (i - 1) % count) for i in range(count)]
 
 
-def all_sum(value, axis):
-    count = lax.axis_size(axis)
-    if count & (count - 1):
-        return lax.psum(value, axis)
-    step = 1
-    while step < count:
-        value = value + lax.ppermute(value, axis, [(i, i ^ step) for i in range(count)])
-        step *= 2
-    return value
+def state_near(scal, base, near, speed, out):
+    step, side = scal[0], scal[1]
+    x = near[0]
+    out[0] = base[0] + step * (x - (0.5 * side) * (x * (speed[...] + 0.5 * x)))
 
 
-def state_update(scal, base, near, far, speed, out):
+def state_far(scal, base, far, speed, out):
     step, side = scal[0], scal[1]
-    u = speed[...]
-    a, b = near[0], far[0]
-    flux = b * (u + 0.5 * b) - a * (u + 0.5 * a)
-    out[0] = base[0] + step * (a + b + (0.5 * side) * flux)
+    x = far[0]
+    out[0] = base[0] + step * (x + (0.5 * side) * (x * (speed[...] + 0.5 * x)))
 
 
-def cot_update(scal, base, near, far, state, speed, out):
+def cot_near(scal, base, near, state, speed, out):
     step, side = scal[0], scal[1]
-    a, b = near[0], far[0]
-    slope = (0.5 * side) * (speed[...] + state[0])
-    out[0] = base[0] + step * (a + b + slope * (a - b))
+    out[0] = base[0] + step * near[0] * (1.0 + (0.5 * side) * (speed[...] + state[0]))
 
 
-def chunk_update(body, scal, base, whole, part, speed, start, rows):
-    width = base.shape[2]
-    block = min(BLOCK_ROWS, rows)
+def cot_far(scal, base, far, state, speed, out):
+    step, side = scal[0], scal[1]
+    out[0] = base[0] + step * far[0] * (1.0 - (0.5 * side) * (speed[...] + state[0]))
+
+
+def add_rows(body, scal, base, part, whole, speed, start):
+    rows, width = part.shape[1:]
+    block = math.gcd(BLOCK_ROWS, rows)
     first = start // block
     full = pl.BlockSpec((1, block, width), lambda i: (0, first + i, 0))
     piece = pl.BlockSpec((1, block, width), lambda i: (0, i, 0))
@@ -66,16 +62,15 @@
         body,
         grid=(rows // block,),
         out_shape=jax.ShapeDtypeStruct(base.shape, base.dtype),
-        in_specs=[pl.BlockSpec(memory_space=pltpu.SMEM), full]
-        + [piece] * len(part)
+        in_specs=[pl.BlockSpec(memory_space=pltpu.SMEM), full, piece]
         + [full] * len(whole)
         + [column],
         out_specs=full,
         input_output_aliases={1: 0},
         cost_estimate=pl.CostEstimate(
-            flops=10 * rows * width, bytes_accessed=4 * rows * width * 5, transcendentals=0
+            flops=10 * rows * width, bytes_accessed=4 * rows * width * 4, transcendentals=0
         ),
-    )(scal, base, *part, *whole, speed)
+    )(scal, base, part, *whole, speed)
 
 
 def local_parts(
@@ -117,18 +112,9 @@
     rows = checkpoint.shape[1]
     near, far = on_pairs(count), off_pairs(count)
 
-    def exchange(value, pieces):
-        size = rows // pieces
-        return [
-            (
-                lax.ppermute(value[:, n * size : (n + 1) * size], "ax", far),
-                lax.ppermute(value[:, n * size : (n + 1) * size], "ax", near),
-            )
-            for n in range(pieces)
-        ]
-
-    state_halo = exchange(checkpoint, STATE_CHUNKS)
-    cot_halo = exchange(cotangent, COT_CHUNKS)
+    cot_far_rows = lax.ppermute(cotangent, "ax", far)
+    cot_near_rows = lax.ppermute(cotangent, "ax", near)
+    state_near_rows = lax.ppermute(checkpoint, "ax", near)
 
     step_size = section_size(substep)
     patches = amplitudes.shape[0]
@@ -136,23 +122,27 @@
     scal = jnp.stack([step_size, side])
     speed = axial_speed[:, None]
 
+    late, cot_near_rows = lax.optimization_barrier((checkpoint, cot_near_rows))
+    edges = [rows * n // STATE_PARTS for n in STATE_CUTS]
+    state_far_rows = [
+        lax.ppermute(late[:, low:high], "ax", far) for low, high in zip(edges, edges[1:])
+    ]
+
     edge_rows = cotangent[:, -1, :].reshape(-1)
     binned = jax.ops.segment_sum(edge_rows, patch_ids.reshape(-1), num_segments=patches)
     total_cells = checkpoint.shape[0] * count * checkpoint.shape[2]
     norm_factor = (patches / total_cells) ** 0.5
-    gradient = all_sum(step_size * radial_diffusion[-1] * binned, "ax") * norm_factor
+    gradient = lax.all_gather(step_size * radial_diffusion[-1] * binned, "ax")
+    gradient = jnp.sum(gradient, axis=0) * norm_factor
 
     advanced, adjoint = local_parts(
         checkpoint, cotangent, amplitudes, patch_ids, radial_diffusion, azimuth_diffusion, step_size
     )
-    size = rows // STATE_CHUNKS
-    for n, (b, a) in enumerate(state_halo):
-        advanced = chunk_update(state_update, scal, advanced, [], [a, b], speed, n * size, size)
-    size = rows // COT_CHUNKS
-    for n, (b, a) in enumerate(cot_halo):
-        adjoint = chunk_update(
-            cot_update, scal, adjoint, [checkpoint], [a, b], speed, n * size, size
-        )
+    adjoint = add_rows(cot_near, scal, adjoint, cot_near_rows, [checkpoint], speed, 0)
+    advanced = add_rows(state_near, scal, advanced, state_near_rows, [], speed, 0)
+    adjoint = add_rows(cot_far, scal, adjoint, cot_far_rows, [checkpoint], speed, 0)
+    for low, part in zip(edges, state_far_rows):
+        advanced = add_rows(state_far, scal, advanced, part, [], speed, low)
     return (advanced, adjoint, gradient)
 
 

time: 132 us -> 128 us (0.970)
  waiting for transfers between devices: 48.4 us -> 14.7 us
  blocking collectives: 0 us -> 21.6 us
  starting transfers between devices: 19.1 us -> 8.02 us
  Pallas kernels: 17.6 us -> 28.1 us
  local copies, waits for them, and re-layouts: 19.5 us -> 27.8 us
    ppermute x14 -> x5, waiting for transfers between devices: 48.4 us -> 14.7 us  [the longest x2 14.7 us: local(): lax.ppermute(late[:, low:high], 'ax', far)]
    all_gather x0 -> x1, blocking collectives: none -> 21.6 us  [local(): gradient = lax.all_gather(step_size * radial_diffusion[-1] * binned, 'ax')]
    ppermute x14 -> x5, starting transfers between devices: 19.1 us -> 8.02 us  [the longest x1 3.47 us: local(): state_near_rows = lax.ppermute(checkpoint, 'ax', near)]
    pallas_call x5, Pallas kernels: 17.6 us -> 28.1 us  [add_rows(): pl.pallas_call(body, grid=(rows // block,), out_shape=jax.ShapeDtypeStruc...]
    slice x2, local copies, waits for them, and re-layouts: 0.99 us -> 4.55 us  [local_parts(): jnp.roll(cotangent, -1, 2)]
    slice x1, local copies, waits for them, and re-layouts: 0.48 us -> 2.86 us  [local_parts(): weighted[:, 1:, :]]
    slice x2, local copies, waits for them, and re-layouts: 3.22 us -> 5.54 us  [local_parts(): jnp.roll(checkpoint, -1, 2)]
    slice x2 -> x3, local copies, waits for them, and re-layouts: 3.6 us -> 1.94 us  [the longest x2 1.35 us: local(): late[:, low:high]]
  transfers between devices with their start and end apart: 14 -> 5, of which waited for: 6 -> 2; matrix products, arithmetic and copies ran while one was open for 31% -> 40% of each run, Pallas kernels for 8% -> 21%
where the time goes in v2:
time: 128 us; the launch traced here: 127 us
  Pallas kernels  28.1 us (22%)
  local copies, waits for them, and re-layouts  27.8 us (22%)
  other arithmetic  24 us (19%)
  blocking collectives  21.6 us (17%)
  waiting for transfers between devices  14.7 us (11%)
  starting transfers between devices  8.02 us (6%)
  between operations  2.69 us (2%)
    pallas_call x5, Pallas kernels, add_rows(): pl.pallas_call(body, grid=(rows // block,), out_shape=jax.ShapeDtypeStruc...  28.1 us
    all_gather x1, blocking collectives, local(): gradient = lax.all_gather(step_size * radial_diffusion[-1] * binned, 'ax')  21.6 us
    ppermute x2, waiting for transfers between devices, local(): lax.ppermute(late[:, low:high], 'ax', far)  14.7 us
    scatter-add x1, other arithmetic, local(): jax.ops.segment_sum(edge_rows, patch_ids.reshape(-1), num_segments=patches)  11.1 us
    gather x1, local copies, waits for them, and re-layouts, local_parts(): wall_value = jnp.take(amplitudes, patch_ids, axis=0)  9.46 us
    mul x1, other arithmetic, local_parts(): weighted = rd * cotangent  6.44 us
    slice x2, local copies, waits for them, and re-layouts, local_parts(): jnp.roll(checkpoint, -1, 2)  5.54 us
    slice x2, local copies, waits for them, and re-layouts, local_parts(): jnp.roll(cotangent, -1, 2)  4.55 us
  transfers between devices with their start and end apart: 5, of which 2 were waited for; matrix products, arithmetic and copies ran while one was open for 40% of the time, Pallas kernels for 21%

profile of v2, /device:TPU:1, one launch (start us, length us, event | category | flops | bytes accessed | tf_op | source)
XLA Modules:
  0.0 126.8 jit_solution(13817333426685400973)
XLA Ops:
  0.6 0.0 copy-start
  0.6 0.0 copy-start.11
  0.7 0.0 copy-start.1
  0.7 0.0 copy-start.7
  0.7 0.0 copy-start.8
  0.7 0.1 collective-permute-start.1
  0.8 2.6 %collective-permute-start.4 = (f32[1,384,1536]{2,1,0:T(8,128)}, f32[1,384,1536]{2,1,0:T(8,128)}, u32[]{:S(2)}, u32[]{:S(2)}) collective-permute-start(f32[1,384,1536]{2,1,0:T(8,128)} %param.10), channel_id=1, source_target_pairs={{0,15},{1,2},{2,1},{3,4},{4,3},{5,6},{6,5},{7,8},{8,7},{9,10},{10,... | collective-permute-start | bytes 7077896 | tf_op jit(solution)/shard_map/ppermute | solution.py:115
  3.4 3.5 %collective-permute-start = (f32[1,384,1536]{2,1,0:T(8,128)}, f32[1,384,1536]{2,1,0:T(8,128)}, u32[]{:S(2)}, u32[]{:S(2)}) collective-permute-start(f32[1,384,1536]{2,1,0:T(8,128)} %state.3), channel_id=1, source_target_pairs={{0,1},{1,0},{2,3},{3,2},{4,5},{5,4},{6,7},{7,6},{8,9},{9,8},{10,11... | collective-permute-start | bytes 7077896 | tf_op jit(solution)/shard_map/ppermute | solution.py:117
  6.9 5.4 %fusion.25 = (f32[1,384,1535]{2,1,0:T(8,128)}, f32[1,384,1535]{2,1,0:T(8,128)}) fusion(f32[1,384,1536]{2,1,0:T(8,128)} %state.3), kind=kLoop, calls=%fused_computation.42 | loop fusion | bytes 9431040 | tf_op jit(solution)/shard_map/jit(_roll_static)/slice | solution.py:86
  12.3 0.0 copy-done.1
  12.3 0.1 fusion.26
  12.5 0.8 slice_reduce_fusion
  13.9 0.0 copy-done.7
  14.0 0.0 copy-done.8
  14.0 0.6 slice.92
  14.6 0.0 copy-done.11
  14.6 0.6 fusion.16
  15.2 9.5 %gather_fusion = f32[1536]{0:T(1024)S(1)} fusion(f32[256]{0:T(256)S(1)} %copy-done, s32[2048]{0:T(1024)S(1)} %pad_clamp_fusion), kind=kCustom, calls=%fused_computation | custom fusion | bytes 18432 | tf_op jit(solution)/shard_map/jit(_take)/gather | solution.py:82
  25.9 11.1 %scatter_custom_fusion = f32[256]{0:T(256)S(1)} fusion(s32[1536]{0:T(1024)S(1)} %get-tuple-element.7, f32[1536]{0:T(1024)S(1)} %slice_reduce_fusion, f32[]{:T(128)} %constant.19.clone.1), kind=kCustom, calls=%fused_computation.33 | custom fusion | flops 1536 | bytes 1028 | tf_op jit(solution)/shard_map/scatter-add | solution.py:132
  37.1 0.0 copy-done.9
  37.1 6.4 %broadcast_multiply_fusion = (f32[1,384,1536]{2,1,0:T(8,128)S(1)}, f32[1,384,1536]{2,1,0:T(8,128)}) fusion(f32[1,384,1536]{2,1,0:T(8,128)} %param.10, f32[384]{0:T(512)S(1)} %copy-done.8, f32[1,384,1536]{2,1,0:T(8,128)S(1)} %copy-done.1, f32[1,384,1]{2,1,0:T(8,128)S(1)} %get-tuple-element.19, f32[1,384,1535]{2,1,0:T(8,128)} %get-tuple-element.17, ...), kind=kLoop, calls=%fused_computation.23 | loop fusion | flops 10027008 | bytes 14171140 | tf_op jit(solution)/shard_map/mul | solution.py:89
  43.5 2.9 %fusion.21 = (f32[1,383,1536]{2,1,0:T(8,128)}, f32[1,383,1536]{2,1,0:T(8,128)}) fusion(f32[1,384,1536]{2,1,0:T(8,128)S(1)} %get-tuple-element.23), kind=kLoop, calls=%fused_computation.38 | loop fusion | bytes 9412608 | tf_op jit(solution)/shard_map/slice | solution.py:91
  46.4 21.6 %all-gather.1 = f32[16,1,256]{2,1,0:T(1,128)S(1)} all-gather(f32[1,1,256]{2,1,0:T(1,128)S(1)} %bitcast.8), channel_id=2, replica_groups=mesh['case'=2,'ax'=16] {'ax'}, dimensions={0}, use_global_device_ids=true | all-gather | bytes 17408 | tf_op jit(solution)/shard_map/all_gather | solution.py:135
  68.0 0.8 fusion.24
  68.8 0.0 collective-permute-done.1.near
  68.8 1.3 %slice.82 = f32[1,288,1536]{2,1,0:T(8,128)} slice(f32[1,384,1536]{2,1,0:T(8,128)S(1)} %copy-done.1), slice={[0:1], [0:288], [0:1536]} | slice | bytes 3538944 | tf_op jit(solution)/shard_map/slice | solution.py:128
  70.1 1.0 collective-permute-start.2
  71.0 0.6 broadcast_multiply_fusion.1
  71.6 0.8 broadcast_in_dim.25.speed
  72.4 1.2 pad_maximum_fusion.3.scal
  73.6 1.1 fusion.23
  74.7 0.0 copy-start.2
  74.8 0.0 copy-start.4
  74.8 0.0 copy-start.5
  74.8 3.4 %fusion.22 = (f32[1,384,1535]{2,1,0:T(8,128)S(1)}, f32[1,384,1535]{2,1,0:T(8,128)S(1)}) fusion(f32[1,384,1536]{2,1,0:T(8,128)} %param.10), kind=kLoop, calls=%fused_computation.39 | loop fusion | bytes 9431040 | tf_op jit(solution)/shard_map/jit(_roll_static)/slice | solution.py:95
  78.2 0.9 collective-permute-start.3
  79.1 0.2 copy-done.5
  79.3 3.9 %fusion.12.base = f32[1,384,1536]{2,1,0:T(8,128)} fusion(f32[1,384,1536]{2,1,0:T(8,128)S(1)} %copy-done.2, f32[1,383,1536]{2,1,0:T(8,128)S(1)} %copy-done.5, f32[1,1,768]{2,1,0:T(1,128)S(1)} %get-tuple-element.16, f32[1,1,768]{2,1,0:T(1,128)S(1)} %get-tuple-element.15, f32[1,384,1535]{2,1,0:T(8,128)S(1)} %get-tuple-element.12, ...), kind=kLoop, calls=%fused_computation.19 | loop fusion | flops 9437184 | bytes 14152708 | tf_op jit(solution)/shard_map/add | solution.py:97
  83.2 7.0 %shard_map.115.base = f32[1,384,1536]{2,1,0:T(8,128)} custom-call(f32[2]{0:T(128)} %pad_maximum_fusion.3.scal, f32[1,384,1536]{2,1,0:T(8,128)} %fusion.12.base, f32[1,384,1536]{2,1,0:T(8,128)} %collective-permute-done.1.near, f32[1,384,1536]{2,1,0:T(8,128)} %state.3, f32[384,1]{1,0:T(8,128)} %broadcast_in_dim.25.speed), custom_call_target="tpu_custom_call", output_to_operand_aliasing={{}: (1, {})} | custom-call | flops 5898240 | bytes 9437184 | tf_op jit(solution)/shard_map/pallas_call | solution.py:61
  90.2 0.0 collective-permute-done.4.far
  90.2 7.0 %shard_map.116 = f32[1,384,1536]{2,1,0:T(8,128)} custom-call(f32[2]{0:T(128)} %pad_maximum_fusion.3.scal, f32[1,384,1536]{2,1,0:T(8,128)} %shard_map.115.base, f32[1,384,1536]{2,1,0:T(8,128)} %collective-permute-done.4.far, f32[1,384,1536]{2,1,0:T(8,128)} %state.3, f32[384,1]{1,0:T(8,128)} %broadcast_in_dim.25.speed), custom_call_target="tpu_custom_call", output_to_operand_aliasing={{}: (1, {})} | custom-call | flops 5898240 | bytes 9437184 | tf_op jit(solution)/shard_map/pallas_call | solution.py:61
  97.2 0.0 collective-permute-done.near
  97.2 6.7 %shard_map.112.base = f32[1,384,1536]{2,1,0:T(8,128)} custom-call(f32[2]{0:T(128)} %pad_maximum_fusion.3.scal, f32[1,384,1536]{2,1,0:T(8,128)} %get-tuple-element.24.base, f32[1,384,1536]{2,1,0:T(8,128)} %collective-permute-done.near, f32[384,1]{1,0:T(8,128)} %broadcast_in_dim.25.speed), custom_call_target="tpu_custom_call", output_to_operand_aliasing={{}: (1, {})} | custom-call | flops 5898240 | bytes 9437184 | tf_op jit(solution)/shard_map/pallas_call | solution.py:61
  103.9 13.7 %collective-permute-done.2.far = f32[1,288,1536]{2,1,0:T(8,128)} collective-permute-done((f32[1,288,1536]{2,1,0:T(8,128)}, f32[1,288,1536]{2,1,0:T(8,128)}, u32[]{:S(2)}, u32[]{:S(2)}) %collective-permute-start.2) | collective-permute-done | bytes 1769504 | tf_op jit(solution)/shard_map/ppermute | solution.py:128
  117.6 5.3 %shard_map.113.base = f32[1,384,1536]{2,1,0:T(8,128)} custom-call(f32[2]{0:T(128)} %pad_maximum_fusion.3.scal, f32[1,384,1536]{2,1,0:T(8,128)} %shard_map.112.base, f32[1,288,1536]{2,1,0:T(8,128)} %collective-permute-done.2.far, f32[384,1]{1,0:T(8,128)} %broadcast_in_dim.25.speed), custom_call_target="tpu_custom_call", output_to_operand_aliasing={{}: (1, {})} | custom-call | flops 4423680 | bytes 7077888 | tf_op jit(solution)/shard_map/pallas_call | solution.py:61
  122.9 0.9 collective-permute-done.3.far
  123.8 0.8 copy-done.6
  124.7 2.1 %shard_map.114 = f32[1,384,1536]{2,1,0:T(8,128)} custom-call(f32[2]{0:T(128)} %pad_maximum_fusion.3.scal, f32[1,384,1536]{2,1,0:T(8,128)} %shard_map.113.base, f32[1,96,1536]{2,1,0:T(8,128)} %copy-done.6, f32[384,1]{1,0:T(8,128)} %broadcast_in_dim.25.speed), custom_call_target="tpu_custom_call", output_to_operand_aliasing={{}: (1, {})} | custom-call | flops 1474560 | bytes 2359296 | tf_op jit(solution)/shard_map/pallas_call | solution.py:61
  (16 shorter events, 0.2 us)
Async XLA Ops:
  0.6 14.6 %copy-start = (f32[256]{0:T(256)S(1)}, f32[256]{0:T(256)}, u32[]{:S(2)}) copy-start(f32[256]{0:T(256)} %param.11) | copy-start | bytes 3076
  0.6 14.0 %copy-start.11 = (f32[3]{0:T(128)S(1)}, f32[3]{0:T(128)}, u32[]{:S(2)}) copy-start(f32[3]{0:T(128)} %constant.55) | copy-start | bytes 40
  0.7 11.7 %copy-start.1 = (f32[1,384,1536]{2,1,0:T(8,128)S(1)}, f32[1,384,1536]{2,1,0:T(8,128)}, u32[]{:S(2)}) copy-start(f32[1,384,1536]{2,1,0:T(8,128)} %state.3) | copy-start | bytes 7077892
  0.7 13.3 %copy-start.7 = (s32[1,1536]{1,0:T(1,128)S(1)}, s32[1,1536]{1,0:T(1,128)}, u32[]{:S(2)}) copy-start(s32[1,1536]{1,0:T(1,128)} %param.12) | copy-start | bytes 18436
  0.7 13.3 %copy-start.8 = (f32[384]{0:T(512)S(1)}, f32[384]{0:T(512)}, u32[]{:S(2)}) copy-start(f32[384]{0:T(512)} %param.15) | copy-start | bytes 4612
  0.7 68.1 %collective-permute-start.1 = (f32[1,384,1536]{2,1,0:T(8,128)}, f32[1,384,1536]{2,1,0:T(8,128)}, u32[]{:S(2)}, u32[]{:S(2)}) collective-permute-start(f32[1,384,1536]{2,1,0:T(8,128)} %param.10), channel_id=1, source_target_pairs={{0,1},{1,0},{2,3},{3,2},{4,5},{5,4},{6,7},{7,6},{8,9},{9,8},{10,11... | collective-permute-start | bytes 7077896 | tf_op jit(solution)/shard_map/ppermute | solution.py:116
  0.8 89.4 %collective-permute-start.4 = (f32[1,384,1536]{2,1,0:T(8,128)}, f32[1,384,1536]{2,1,0:T(8,128)}, u32[]{:S(2)}, u32[]{:S(2)}) collective-permute-start(f32[1,384,1536]{2,1,0:T(8,128)} %param.10), channel_id=1, source_target_pairs={{0,15},{1,2},{2,1},{3,4},{4,3},{5,6},{6,5},{7,8},{8,7},{9,10},{10,... | collective-permute-start | bytes 7077896 | tf_op jit(solution)/shard_map/ppermute | solution.py:115
  3.4 93.8 %collective-permute-start = (f32[1,384,1536]{2,1,0:T(8,128)}, f32[1,384,1536]{2,1,0:T(8,128)}, u32[]{:S(2)}, u32[]{:S(2)}) collective-permute-start(f32[1,384,1536]{2,1,0:T(8,128)} %state.3), channel_id=1, source_target_pairs={{0,1},{1,0},{2,3},{3,2},{4,5},{5,4},{6,7},{7,6},{8,9},{9,8},{10,11... | collective-permute-start | bytes 7077896 | tf_op jit(solution)/shard_map/ppermute | solution.py:117
  15.2 21.9 %copy-start.9 = (f32[384]{0:T(512)S(1)}, f32[384]{0:T(512)}, u32[]{:S(2)}) copy-start(f32[384]{0:T(512)} %param.16) | copy-start | bytes 4612
  43.5 2.9 %copy-start.3 = (f32[1,384,1536]{2,1,0:T(8,128)}, f32[1,384,1536]{2,1,0:T(8,128)S(1)}, u32[]{:S(2)}) copy-start(f32[1,384,1536]{2,1,0:T(8,128)S(1)} %get-tuple-element.23) | copy-start | bytes 7077892
  46.4 25.2 %copy-start.10 = (f32[384]{0:T(512)S(1)}, f32[384]{0:T(512)}, u32[]{:S(2)}) copy-start(f32[384]{0:T(512)} %param.14) | copy-start | bytes 4612
  70.1 47.5 %collective-permute-start.2 = (f32[1,288,1536]{2,1,0:T(8,128)}, f32[1,288,1536]{2,1,0:T(8,128)}, u32[]{:S(2)}, u32[]{:S(2)}) collective-permute-start(f32[1,288,1536]{2,1,0:T(8,128)} %slice.82), channel_id=1, source_target_pairs={{0,15},{1,2},{2,1},{3,4},{4,3},{5,6},{6,5},{7,8},{8,7},{9,10},{10,... | collective-permute-start | bytes 5308424 | tf_op jit(solution)/shard_map/ppermute | solution.py:128
  74.7 4.4 %copy-start.2 = (f32[1,384,1536]{2,1,0:T(8,128)S(1)}, f32[1,384,1536]{2,1,0:T(8,128)}, u32[]{:S(2)}) copy-start(f32[1,384,1536]{2,1,0:T(8,128)} %param.10) | copy-start | bytes 7077892
  74.8 4.4 %copy-start.4 = (f32[1,383,1536]{2,1,0:T(8,128)S(1)}, f32[1,383,1536]{2,1,0:T(8,128)}, u32[]{:S(2)}) copy-start(f32[1,383,1536]{2,1,0:T(8,128)} %get-tuple-element.9) | copy-start | bytes 7059460
  74.8 4.5 %copy-start.5 = (f32[1,383,1536]{2,1,0:T(8,128)S(1)}, f32[1,383,1536]{2,1,0:T(8,128)}, u32[]{:S(2)}) copy-start(f32[1,383,1536]{2,1,0:T(8,128)} %get-tuple-element.10) | copy-start | bytes 7059460
  78.2 45.6 %collective-permute-start.3 = (f32[1,96,1536]{2,1,0:T(8,128)S(1)}, f32[1,96,1536]{2,1,0:T(8,128)S(1)}, u32[]{:S(2)}, u32[]{:S(2)}) collective-permute-start(f32[1,96,1536]{2,1,0:T(8,128)S(1)} %slice.83), channel_id=1, source_target_pairs={{0,15},{1,2},{2,1},{3,4},{4,3},{5,6},{6,5},{7,8},{8,7},{9,10},{10,... | collective-permute-start | bytes 1769480 | tf_op jit(solution)/shard_map/ppermute | solution.py:128
  123.8 0.8 copy-start.6

commit v3 on v2

v3 whole, which is shorter than its diff:
```python
import math

import jax
import jax.numpy as jnp
from jax import lax
from jax.experimental import pallas as pl
from jax.experimental.pallas import tpu as pltpu
from jax.sharding import PartitionSpec as P

time_step = 0.6
dissipation = 2.0

STATE_PARTS = 4
STATE_CUTS = (0, 3, 4)
LOCAL_ROWS = 64
ADD_ROWS = 96
SUB = 8


def section_size(substep):
    section_table = jnp.array([1.0 / 3.0, 15.0 / 16.0, 8.0 / 15.0], jnp.float32) * time_step
    selector = (jnp.arange(3, dtype=jnp.int32) == substep[0]).astype(jnp.float32)
    return jnp.sum(section_table * selector)


def on_pairs(count):
    return [(i, i ^ 1) for i in range(count)]


def off_pairs(count):
    return [(i, (i + 1) % count if i % 2 else (i - 1) % count) for i in range(count)]


def wall_kernel(ids, amplitudes, edge, wall, bins):
    patches, cells = amplitudes.shape[1], ids.shape[1]
    patch = lax.broadcasted_iota(jnp.int32, (patches, cells), 0)
    hit = jnp.where(patch == ids[...], 1.0, 0.0).astype(jnp.float32)
    values = jnp.broadcast_to(amplitudes[...], (SUB, patches))
    wall[...] = lax.dot_general(
        values,
        hit,
        (((1,), (0,)), ((), ())),
        precision=lax.Precision.HIGHEST,
        preferred_element_type=jnp.float32,
    )[:1]
    bins[...] = lax.dot_general(
        edge[0],
        hit,
        (((1,), (1,)), ((), ())),
        precision=lax.Precision.HIGHEST,
        preferred_element_type=jnp.float32,
    )[SUB - 1 :]


def wall_and_bins(patch_ids, amplitudes, cotangent):
    rows, cells = cotangent.shape[1:]
    patches = amplitudes.shape[0]
    return pl.pallas_call(
        wall_kernel,
        grid=(1,),
        out_shape=(
            jax.ShapeDtypeStruct((1, cells), jnp.float32),
            jax.ShapeDtypeStruct((1, patches), jnp.float32),
        ),
        in_specs=[
            pl.BlockSpec((1, cells), lambda i: (0, 0)),
            pl.BlockSpec((1, patches), lambda i: (0, 0)),
            pl.BlockSpec((1, SUB, cells), lambda i: (0, rows // SUB - 1, 0)),
        ],
        out_specs=(
            pl.BlockSpec((1, cells), lambda i: (0, 0)),
            pl.BlockSpec((1, patches), lambda i: (0, 0)),
        ),
        compiler_params=pltpu.CompilerParams(vmem_limit_bytes=40 << 20),
    )(patch_ids, amplitudes[None], cotangent)


def local_kernel(scal, q, q_up, q_down, q_near, c, c_up, c_down, c_near, wall, coef, q_out, c_out):
    block, width = q.shape[1:]
    step, side = scal[0], scal[1]
    here, last = pl.program_id(0), pl.num_programs(0) - 1
    u, rd, ad = coef[:, 0:1], coef[:, 1:2], coef[:, 2:3]
    row = lax.broadcasted_iota(jnp.int32, (block, 1), 0)

    def around(x, up, down):
        above = jnp.where(row == 0, up, pltpu.roll(x, 1, 0))
        below = jnp.where(row == block - 1, down, pltpu.roll(x, block - 1, 0))
        return above, below

    def sides(x):
        return pltpu.roll(x, 1, 1) + pltpu.roll(x, width - 1, 1)

    x = q[0]
    first_row = pltpu.roll(x[:1], width // 2, 1)
    up = jnp.where(here == 0, first_row, q_up[0, SUB - 1 :])
    down = jnp.where(here == last, wall[...], q_down[0, :1])
    above, below = around(x, up, down)
    near = q_near[0]
    axial = near - (0.5 * side) * (near * (u + 0.5 * near)) - dissipation * x
    q_out[0] = x + step * (
        axial + rd * (above + below - 2.0 * x) + ad * (sides(x) - 2.0 * x)
    )

    y = c[0]
    weighted = rd * y
    before, after = coef_rows(coef)
    first_row = pltpu.roll(weighted[:1], width // 2, 1)
    up = jnp.where(here == 0, first_row, before * c_up[0, SUB - 1 :])
    down = jnp.where(here == last, 0.0, after * c_down[0, :1])
    above, below = around(weighted, up, down)
    axial = c_near[0] * (1.0 + (0.5 * side) * (u + x)) - dissipation * y
    c_out[0] = y + step * (
        axial + (above + below - 2.0 * weighted) + ad * (sides(y) - 2.0 * y)
    )


def coef_rows(coef):
    return coef[0:1, 3:4], coef[0:1, 4:5]


def local_parts(scal, q, q_near, c, c_near, wall, coef):
    rows, width = q.shape[1:]
    block = math.gcd(LOCAL_ROWS, rows)
    tiles, total = block // SUB, rows // SUB
    full = pl.BlockSpec((1, block, width), lambda i: (0, i, 0))
    up = pl.BlockSpec((1, SUB, width), lambda i: (0, jnp.maximum(i * tiles - 1, 0), 0))
    down = pl.BlockSpec((1, SUB, width), lambda i: (0, jnp.minimum((i + 1) * tiles, total - 1), 0))
    rd = coef[:, 1]
    before, after = jnp.roll(rd, 1), jnp.roll(rd, -block)
    coef = jnp.concatenate([coef, before[:, None], after[:, None]], axis=1)
    shape = jax.ShapeDtypeStruct(q.shape, q.dtype)
    return pl.pallas_call(
        local_kernel,
        grid=(rows // block,),
        out_shape=(shape, shape),
        in_specs=[pl.BlockSpec(memory_space=pltpu.SMEM)]
        + [full, up, down, full] * 2
        + [pl.BlockSpec((1, width), lambda i: (0, 0))]
        + [pl.BlockSpec((block, coef.shape[1]), lambda i: (i, 0))],
        out_specs=(full, full),
        compiler_params=pltpu.CompilerParams(vmem_limit_bytes=40 << 20),
        cost_estimate=pl.CostEstimate(
            flops=50 * rows * width, bytes_accessed=4 * rows * width * 6, transcendentals=0
        ),
    )(scal, q, q, q, q_near, c, c, c, c_near, wall, coef)


def state_far(scal, base, far, coef, out):
    step, side = scal[0], scal[1]
    x = far[0]
    out[0] = base[0] + step * (x + (0.5 * side) * (x * (coef[:, 0:1] + 0.5 * x)))


def state_last(scal, base, far, mine, other, coef, out, gradient):
    state_far(scal, base, far, coef, out)
    gradient[...] = scal[2] * (mine[...] + other[...])


def cot_far(scal, base, far, state, coef, out):
    step, side = scal[0], scal[1]
    out[0] = base[0] + step * far[0] * (1.0 - (0.5 * side) * (coef[:, 0:1] + state[0]))


def add_rows(body, scal, base, part, whole, coef, start, small=()):
    rows, width = part.shape[1:]
    block = math.gcd(ADD_ROWS, rows)
    first = start // block
    full = pl.BlockSpec((1, block, width), lambda i: (0, first + i, 0))
    piece = pl.BlockSpec((1, block, width), lambda i: (0, i, 0))
    column = pl.BlockSpec((block, coef.shape[1]), lambda i: (first + i, 0))
    short = [pl.BlockSpec(x.shape, lambda i: (0, 0)) for x in small]
    shape = jax.ShapeDtypeStruct(base.shape, base.dtype)
    return pl.pallas_call(
        body,
        grid=(rows // block,),
        out_shape=(shape, jax.ShapeDtypeStruct(small[0].shape, base.dtype)) if small else shape,
        in_specs=[pl.BlockSpec(memory_space=pltpu.SMEM), full, piece]
        + short
        + [full] * len(whole)
        + [column],
        out_specs=(full, short[0]) if small else full,
        input_output_aliases={1: 0},
        compiler_params=pltpu.CompilerParams(vmem_limit_bytes=40 << 20),
        cost_estimate=pl.CostEstimate(
            flops=10 * rows * width, bytes_accessed=4 * rows * width * 4, transcendentals=0
        ),
    )(scal, base, part, *small, *whole, coef)


def local(
    checkpoint,
    cotangent,
    amplitudes,
    patch_ids,
    substep,
    axial_speed,
    radial_diffusion,
    azimuth_diffusion,
):
    count = lax.axis_size("ax")
    rows = checkpoint.shape[1]
    patches = amplitudes.shape[0]
    near, far = on_pairs(count), off_pairs(count)
    cot_far_rows = lax.ppermute(cotangent, "ax", far)
    cot_near_rows = lax.ppermute(cotangent, "ax", near)
    state_near_rows = lax.ppermute(checkpoint, "ax", near)

    cot_now, cot_near_rows = lax.optimization_barrier((cotangent, cot_near_rows))
    wall, binned = wall_and_bins(patch_ids, amplitudes, cot_now)

    if count & (count - 1) or count < 4:
        binned = lax.psum(binned, "ax")
        other = jnp.zeros_like(binned)
        late = checkpoint
    else:
        for n in [1] + [1 << n for n in range(2, count.bit_length() - 1)]:
            binned = binned + lax.ppermute(binned, "ax", [(i, i ^ n) for i in range(count)])
        late, binned, state_near_rows = lax.optimization_barrier(
            (checkpoint, binned, state_near_rows)
        )
        other = lax.ppermute(binned, "ax", [(i, i ^ 2) for i in range(count)])

    edges = [rows * n // STATE_PARTS for n in STATE_CUTS]
    state_far_rows = [
        lax.ppermute(late[:, low:high], "ax", far) for low, high in zip(edges, edges[1:])
    ]

    step_size = section_size(substep)
    side = 1.0 - 2.0 * (lax.axis_index("ax") % 2).astype(jnp.float32)
    total_cells = checkpoint.shape[0] * count * checkpoint.shape[2]
    norm_factor = (patches / total_cells) ** 0.5
    scal = jnp.stack([step_size, side, step_size * radial_diffusion[-1] * norm_factor])
    coef = jnp.stack([axial_speed, radial_diffusion, azimuth_diffusion], axis=1)

    advanced, adjoint = local_parts(
        scal, checkpoint, state_near_rows, cotangent, cot_near_rows, wall, coef
    )
    adjoint = add_rows(cot_far, scal, adjoint, cot_far_rows, [checkpoint], coef, 0)
    advanced, adjoint = lax.optimization_barrier((advanced, adjoint))
    for low, part in zip(edges[:-2], state_far_rows[:-1]):
        advanced = add_rows(state_far, scal, advanced, part, [], coef, low)
    advanced, gradient = add_rows(
        state_last, scal, advanced, state_far_rows[-1], [], coef, edges[-2], (binned, other)
    )
    return (advanced, adjoint, gradient[0])


def solution(mesh):
    placed = (
        P(("case", "ax"), None, None),
        P(("case", "ax"), None, None),
        P("case"),
        P(("case", "ax"), None),
        P("case"),
        P(),
        P(),
        P(),
    )
    return jax.shard_map(
        local,
        mesh=mesh,
        in_specs=placed,
        out_specs=(P(("case", "ax"), None, None), P(("case", "ax"), None, None), P("case")),
        check_vma=False,
    )
```

time: 128 us -> 110 us (0.86)
  waiting for transfers between devices: 14.7 us -> 43.6 us
  other arithmetic: 24 us -> 2.04 us
  blocking collectives: 21.6 us -> 0 us
  starting transfers between devices: 8.02 us -> 28.5 us
  local copies, waits for them, and re-layouts: 27.8 us -> 12.6 us
  Pallas kernels: 28.1 us -> 19.2 us
    ppermute x0 -> x4, starting transfers between devices: none -> 22.3 us  [the longest x1 17.2 us: local(): other = lax.ppermute(binned, 'ax', [(i, i ^ 2) for i in range(count)])]
    ppermute x1, waiting for transfers between devices: 0.01 us -> 21.7 us  [local(): cot_far_rows = lax.ppermute(cotangent, 'ax', far)]
    all_gather x1 -> x0, blocking collectives: 21.6 us -> none  [local(): gradient = lax.all_gather(step_size * radial_diffusion[-1] * binned, 'ax')]
    slice x9 -> x3, local copies, waits for them, and re-layouts: 15.1 us -> 0.65 us  [the longest x1 0.58 us: local(): radial_diffusion[-1]]
    scatter-add x1 -> x0, other arithmetic: 11.1 us -> none  [local(): jax.ops.segment_sum(edge_rows, patch_ids.reshape(-1), num_segments=patches)]
    gather x1 -> x0, local copies, waits for them, and re-layouts: 9.46 us -> none  [local_parts(): wall_value = jnp.take(amplitudes, patch_ids, axis=0)]
    pallas_call x5, Pallas kernels: 28.1 us -> 19.2 us  [the longest x3 10.9 us: add_rows(): pl.pallas_call(body, grid=(rows // block,), out_shape=(shape, jax.ShapeDt...]
    unnamed x24 -> x26, local copies, waits for them, and re-layouts: 1.03 us -> 9.46 us
  transfers between devices with their start and end apart: 5 -> 9, of which waited for: 2 -> 8; matrix products, arithmetic and copies ran while one was open for 40% -> 5% of each run, Pallas kernels for 21% -> 16%
where the time goes in v3:
time: 110 us; the launch traced here: 108 us
  waiting for transfers between devices  43.6 us (40%)
  starting transfers between devices  28.5 us (26%)
  Pallas kernels  19.2 us (17%)
  local copies, waits for them, and re-layouts  12.6 us (11%)
  between operations  2.6 us (2%)
  other arithmetic  2.04 us (2%)
    ppermute x1, waiting for transfers between devices, local(): cot_far_rows = lax.ppermute(cotangent, 'ax', far)  21.7 us
    ppermute x1, starting transfers between devices, local(): other = lax.ppermute(binned, 'ax', [(i, i ^ 2) for i in range(count)])  17.2 us
    ppermute x2, waiting for transfers between devices, local(): lax.ppermute(late[:, low:high], 'ax', far)  15 us
    pallas_call x3, Pallas kernels, add_rows(): pl.pallas_call(body, grid=(rows // block,), out_shape=(shape, jax.ShapeDt...  10.9 us
    unnamed x26, local copies, waits for them, and re-layouts  9.46 us
    pallas_call x1, Pallas kernels, local_parts(): pl.pallas_call(local_kernel, grid=(rows // block,), out_shape=(shape, sha...  6.09 us
    ppermute x3, starting transfers between devices, local(): lax.ppermute(binned, 'ax', [(i, i ^ n) for i in range(count)])  5.14 us
    ppermute x3, waiting for transfers between devices, local(): lax.ppermute(binned, 'ax', [(i, i ^ n) for i in range(count)])  3.87 us
  transfers between devices with their start and end apart: 9, of which 8 were waited for; matrix products, arithmetic and copies ran while one was open for 5% of the time, Pallas kernels for 16%

profile of v3, /device:TPU:1, one launch (start us, length us, event | category | flops | bytes accessed | tf_op | source)
XLA Modules:
  0.0 108.5 jit_solution(15203922087215191458)
XLA Ops:
  0.6 0.0 copy-start
  0.6 0.1 collective-permute-start
  0.8 0.5 collective-permute-start.4
  1.2 2.6 %collective-permute-start.5 = (f32[1,384,1536]{2,1,0:T(8,128)}, f32[1,384,1536]{2,1,0:T(8,128)}, u32[]{:S(2)}, u32[]{:S(2)}) collective-permute-start(f32[1,384,1536]{2,1,0:T(8,128)} %c_down.1), channel_id=1, source_target_pairs={{0,15},{1,2},{2,1},{3,4},{4,3},{5,6},{6,5},{7,8},{8,7},{9,10},{10,... | collective-permute-start | bytes 7077896 | tf_op jit(solution)/shard_map/ppermute | solution.py:204
  3.8 1.6 %collective-permute-done.c_near = f32[1,384,1536]{2,1,0:T(8,128)S(1)} collective-permute-done((f32[1,384,1536]{2,1,0:T(8,128)}, f32[1,384,1536]{2,1,0:T(8,128)S(1)}, u32[]{:S(2)}, u32[]{:S(2)}) %collective-permute-start) | collective-permute-done | bytes 2359328 | tf_op jit(solution)/shard_map/ppermute | solution.py:205
  5.5 1.4 %copy-done.3 = f32[1,384,1536]{2,1,0:T(8,128)} copy-done((f32[1,384,1536]{2,1,0:T(8,128)}, f32[1,384,1536]{2,1,0:T(8,128)S(1)}, u32[]{:S(2)}) %copy-start.3) | copy-done | bytes 2359320
  6.9 1.7 %copy-done.1 = f32[1,384,1536]{2,1,0:T(8,128)S(1)} copy-done((f32[1,384,1536]{2,1,0:T(8,128)S(1)}, f32[1,384,1536]{2,1,0:T(8,128)}, u32[]{:S(2)}) %copy-start.1) | copy-done | bytes 2359320
  8.5 0.7 copy-done.7
  9.2 0.7 copy-done.8
  9.9 2.2 %shard_map.112 = (f32[1,1536]{1,0:T(1,128)S(1)}, f32[1,256]{1,0:T(1,128)S(1)}) custom-call(s32[1,1536]{1,0:T(1,128)S(1)} %copy-done.7, f32[1,256]{1,0:T(1,128)S(1)} %bitcast.9, f32[1,384,1536]{2,1,0:T(8,128)S(1)} %copy-done.1), custom_call_target="tpu_custom_call" | custom-call | tf_op jit(solution)/shard_map/pallas_call | solution.py:58
  12.1 1.5 %collective-permute-start.1 = (f32[1,256]{1,0:T(1,128)S(1)}, f32[1,256]{1,0:T(1,128)S(1)}, u32[]{:S(2)}, u32[]{:S(2)}) collective-permute-start(f32[1,256]{1,0:T(1,128)S(1)} %get-tuple-element.17), channel_id=1, source_target_pairs={{0,1},{1,0},{2,3},{3,2},{4,5},{5,4},{6,7},{7,6},{8,9},{9,8},{10,11... | collective-permute-start | bytes 3080 | tf_op jit(solution)/shard_map/ppermute | solution.py:217
  13.6 0.8 collective-permute-done.1
  14.4 1.3 %collective-permute-start.2 = (f32[1,256]{1,0:T(1,128)S(1)}, f32[1,256]{1,0:T(1,128)S(1)}, u32[]{:S(2)}, u32[]{:S(2)}) collective-permute-start(f32[1,256]{1,0:T(1,128)S(1)} %add.14), channel_id=1, source_target_pairs={{0,4},{1,5},{2,6},{3,7},{4,0},{5,1},{6,2},{7,3},{8,12},{9,13},{10,... | collective-permute-start | bytes 3080 | tf_op jit(solution)/shard_map/ppermute | solution.py:217
  15.7 1.6 %collective-permute-done.2 = f32[1,256]{1,0:T(1,128)S(1)} collective-permute-done((f32[1,256]{1,0:T(1,128)S(1)}, f32[1,256]{1,0:T(1,128)S(1)}, u32[]{:S(2)}, u32[]{:S(2)}) %collective-permute-start.2) | collective-permute-done | bytes 1056 | tf_op jit(solution)/shard_map/ppermute | solution.py:217
  17.3 2.3 %collective-permute-start.3 = (f32[1,256]{1,0:T(1,128)S(1)}, f32[1,256]{1,0:T(1,128)S(1)}, u32[]{:S(2)}, u32[]{:S(2)}) collective-permute-start(f32[1,256]{1,0:T(1,128)S(1)} %add.15), channel_id=1, source_target_pairs={{0,8},{1,9},{2,10},{3,11},{4,12},{5,13},{6,14},{7,15},{8,0},{9,1},... | collective-permute-start | bytes 3080 | tf_op jit(solution)/shard_map/ppermute | solution.py:217
  19.7 1.5 %collective-permute-done.3 = f32[1,256]{1,0:T(1,128)S(1)} collective-permute-done((f32[1,256]{1,0:T(1,128)S(1)}, f32[1,256]{1,0:T(1,128)S(1)}, u32[]{:S(2)}, u32[]{:S(2)}) %collective-permute-start.3) | collective-permute-done | bytes 1056 | tf_op jit(solution)/shard_map/ppermute | solution.py:217
  21.1 0.0 copy-start.12
  21.1 0.0 collective-permute-done.4.q_near
  21.2 0.0 copy-done
  21.2 0.0 copy-start.5
  21.2 1.3 %slice.27 = f32[1,288,1536]{2,1,0:T(8,128)} slice(f32[1,384,1536]{2,1,0:T(8,128)S(1)} %copy-done), slice={[0:1], [0:288], [0:1536]} | slice | bytes 3538944 | tf_op jit(solution)/shard_map/slice | solution.py:225
  22.5 3.0 %collective-permute-start.6 = (f32[1,288,1536]{2,1,0:T(8,128)}, f32[1,288,1536]{2,1,0:T(8,128)}, u32[]{:S(2)}, u32[]{:S(2)}) collective-permute-start(f32[1,288,1536]{2,1,0:T(8,128)} %slice.27), channel_id=1, source_target_pairs={{0,15},{1,2},{2,1},{3,4},{4,3},{5,6},{6,5},{7,8},{8,7},{9,10},{10,... | collective-permute-start | bytes 5308424 | tf_op jit(solution)/shard_map/ppermute | solution.py:225
  25.5 0.9 slice.28
  26.4 0.0 copy-done.5
  26.4 0.0 collective-permute-start.7
  26.4 0.0 copy-done.9
  26.4 0.6 slice.23
  27.0 0.1 slice.25
  27.7 0.6 pad_maximum_fusion.1
  28.3 0.0 copy-done.10
  28.3 0.0 copy-done.11
  28.3 0.1 pad_maximum_fusion.2
  28.5 0.1 copy.23.coef
  28.6 0.1 copy.24.coef
  28.8 0.6 fusion
  30.6 0.7 pad_maximum_fusion.3.scal
  31.3 17.2 %collective-permute-start.8 = (f32[1,256]{1,0:T(1,128)S(1)}, f32[1,256]{1,0:T(1,128)S(1)}, u32[]{:S(2)}, u32[]{:S(2)}) collective-permute-start(f32[1,256]{1,0:T(1,128)S(1)} %add.16.mine), channel_id=1, source_target_pairs={{0,2},{1,3},{2,0},{3,1},{4,6},{5,7},{6,4},{7,5},{8,10},{9,11},{10,... | collective-permute-start | bytes 3080 | tf_op jit(solution)/shard_map/ppermute | solution.py:221
  48.5 1.7 %copy-done.2 = f32[1,384,1536]{2,1,0:T(8,128)S(1)} copy-done((f32[1,384,1536]{2,1,0:T(8,128)S(1)}, f32[1,384,1536]{2,1,0:T(8,128)}, u32[]{:S(2)}) %copy-start.2) | copy-done | bytes 2359320
  50.1 1.7 %copy-done.4 = f32[1,384,1536]{2,1,0:T(8,128)S(1)} copy-done((f32[1,384,1536]{2,1,0:T(8,128)S(1)}, f32[1,384,1536]{2,1,0:T(8,128)}, u32[]{:S(2)}) %copy-start.4) | copy-done | bytes 2359320
  51.8 1.7 %copy-done.6 = f32[1,384,1536]{2,1,0:T(8,128)S(1)} copy-done((f32[1,384,1536]{2,1,0:T(8,128)S(1)}, f32[1,384,1536]{2,1,0:T(8,128)}, u32[]{:S(2)}) %copy-start.6) | copy-done | bytes 2359320
  53.5 6.1 %shard_map.113 = (f32[1,384,1536]{2,1,0:T(8,128)}, f32[1,384,1536]{2,1,0:T(8,128)}) custom-call(f32[3]{0:T(128)S(1)} %pad_maximum_fusion.3.scal, f32[1,384,1536]{2,1,0:T(8,128)S(1)} %copy-done, f32[1,384,1536]{2,1,0:T(8,128)S(1)} %copy-done, f32[1,384,1536]{2,1,0:T(8,128)S(1)} %copy-done, f32[1,384,1536]{2,1,0:T(8,128)S(1)} %copy-done.6, ...), custom_call_target="tpu_custom_call" | custom-call | flops 29491200 | bytes 14155776 | tf_op jit(solution)/shard_map/pallas_call | solution.py:132
  59.6 21.7 %collective-permute-done.5.far = f32[1,384,1536]{2,1,0:T(8,128)} collective-permute-done((f32[1,384,1536]{2,1,0:T(8,128)}, f32[1,384,1536]{2,1,0:T(8,128)}, u32[]{:S(2)}, u32[]{:S(2)}) %collective-permute-start.5) | collective-permute-done | bytes 2359328 | tf_op jit(solution)/shard_map/ppermute | solution.py:204
  81.2 4.6 %shard_map.114 = f32[1,384,1536]{2,1,0:T(8,128)} custom-call(f32[3]{0:T(128)S(1)} %pad_maximum_fusion.3.scal, f32[1,384,1536]{2,1,0:T(8,128)} %get-tuple-element.22.base, f32[1,384,1536]{2,1,0:T(8,128)} %collective-permute-done.5.far, f32[1,384,1536]{2,1,0:T(8,128)S(1)} %copy-done, f32[384,3]{1,0:T(8,128)S(1)} %copy.24.coef), custom_call_target="tpu_custom_call", output_to_operand_aliasing={{}: (1, {})} | custom-call | flops 5898240 | bytes 9437184 | tf_op jit(solution)/shard_map/pallas_call | solution.py:173
  85.8 14.4 %collective-permute-done.6.far = f32[1,288,1536]{2,1,0:T(8,128)} collective-permute-done((f32[1,288,1536]{2,1,0:T(8,128)}, f32[1,288,1536]{2,1,0:T(8,128)}, u32[]{:S(2)}, u32[]{:S(2)}) %collective-permute-start.6) | collective-permute-done | bytes 1769504 | tf_op jit(solution)/shard_map/ppermute | solution.py:225
  100.2 4.2 %shard_map.115.base = f32[1,384,1536]{2,1,0:T(8,128)} custom-call(f32[3]{0:T(128)S(1)} %pad_maximum_fusion.3.scal, f32[1,384,1536]{2,1,0:T(8,128)} %get-tuple-element.23.base, f32[1,288,1536]{2,1,0:T(8,128)} %collective-permute-done.6.far, f32[384,3]{1,0:T(8,128)S(1)} %copy.24.coef), custom_call_target="tpu_custom_call", output_to_operand_aliasing={{}: (1, {})} | custom-call | flops 4423680 | bytes 7077888 | tf_op jit(solution)/shard_map/pallas_call | solution.py:173
  104.4 1.4 %collective-permute-done.8.other = f32[1,256]{1,0:T(1,128)S(1)} collective-permute-done((f32[1,256]{1,0:T(1,128)S(1)}, f32[1,256]{1,0:T(1,128)S(1)}, u32[]{:S(2)}, u32[]{:S(2)}) %collective-permute-start.8) | collective-permute-done | bytes 1056 | tf_op jit(solution)/shard_map/ppermute | solution.py:221
  105.8 0.6 collective-permute-done.7.far
  106.4 2.1 %shard_map.116 = (f32[1,384,1536]{2,1,0:T(8,128)}, f32[1,256]{1,0:T(1,128)}) custom-call(f32[3]{0:T(128)S(1)} %pad_maximum_fusion.3.scal, f32[1,384,1536]{2,1,0:T(8,128)} %shard_map.115.base, f32[1,96,1536]{2,1,0:T(8,128)S(1)} %collective-permute-done.7.far, f32[1,256]{1,0:T(1,128)S(1)} %add.16.mine, ...), custom_call_target="tpu_custom_call", output_to_operand_aliasing={{0}: (1, {})} | custom-call | flops 1474560 | bytes 2359296 | tf_op jit(solution)/shard_map/pallas_call | solution.py:173
  (22 shorter events, 0.1 us)
Async XLA Ops:
  0.6 20.5 %copy-start = (f32[1,384,1536]{2,1,0:T(8,128)S(1)}, f32[1,384,1536]{2,1,0:T(8,128)}, u32[]{:S(2)}) copy-start(f32[1,384,1536]{2,1,0:T(8,128)} %state.1) | copy-start | bytes 7077892
  0.6 4.8 %collective-permute-start = (f32[1,384,1536]{2,1,0:T(8,128)}, f32[1,384,1536]{2,1,0:T(8,128)S(1)}, u32[]{:S(2)}, u32[]{:S(2)}) collective-permute-start(f32[1,384,1536]{2,1,0:T(8,128)} %c_down.1), channel_id=1, source_target_pairs={{0,1},{1,0},{2,3},{3,2},{4,5},{5,4},{6,7},{7,6},{8,9},{9,8},{10,11... | collective-permute-start | bytes 7077896 | tf_op jit(solution)/shard_map/ppermute | solution.py:205
  0.8 20.4 %collective-permute-start.4 = (f32[1,384,1536]{2,1,0:T(8,128)}, f32[1,384,1536]{2,1,0:T(8,128)S(1)}, u32[]{:S(2)}, u32[]{:S(2)}) collective-permute-start(f32[1,384,1536]{2,1,0:T(8,128)} %state.1), channel_id=1, source_target_pairs={{0,1},{1,0},{2,3},{3,2},{4,5},{5,4},{6,7},{7,6},{8,9},{9,8},{10,11... | collective-permute-start | bytes 7077896 | tf_op jit(solution)/shard_map/ppermute | solution.py:206
  1.2 80.0 %collective-permute-start.5 = (f32[1,384,1536]{2,1,0:T(8,128)}, f32[1,384,1536]{2,1,0:T(8,128)}, u32[]{:S(2)}, u32[]{:S(2)}) collective-permute-start(f32[1,384,1536]{2,1,0:T(8,128)} %c_down.1), channel_id=1, source_target_pairs={{0,15},{1,2},{2,1},{3,4},{4,3},{5,6},{6,5},{7,8},{8,7},{9,10},{10,... | collective-permute-start | bytes 7077896 | tf_op jit(solution)/shard_map/ppermute | solution.py:204
  5.5 1.4 %copy-start.3 = (f32[1,384,1536]{2,1,0:T(8,128)}, f32[1,384,1536]{2,1,0:T(8,128)S(1)}, u32[]{:S(2)}) copy-start(f32[1,384,1536]{2,1,0:T(8,128)S(1)} %collective-permute-done.c_near) | copy-start | bytes 7077892
  6.9 1.7 %copy-start.1 = (f32[1,384,1536]{2,1,0:T(8,128)S(1)}, f32[1,384,1536]{2,1,0:T(8,128)}, u32[]{:S(2)}) copy-start(f32[1,384,1536]{2,1,0:T(8,128)} %c_down.1) | copy-start | bytes 7077892
  8.5 0.7 copy-start.7
  9.2 0.7 copy-start.8
  12.1 2.3 %collective-permute-start.1 = (f32[1,256]{1,0:T(1,128)S(1)}, f32[1,256]{1,0:T(1,128)S(1)}, u32[]{:S(2)}, u32[]{:S(2)}) collective-permute-start(f32[1,256]{1,0:T(1,128)S(1)} %get-tuple-element.17), channel_id=1, source_target_pairs={{0,1},{1,0},{2,3},{3,2},{4,5},{5,4},{6,7},{7,6},{8,9},{9,8},{10,11... | collective-permute-start | bytes 3080 | tf_op jit(solution)/shard_map/ppermute | solution.py:217
  14.4 2.9 %collective-permute-start.2 = (f32[1,256]{1,0:T(1,128)S(1)}, f32[1,256]{1,0:T(1,128)S(1)}, u32[]{:S(2)}, u32[]{:S(2)}) collective-permute-start(f32[1,256]{1,0:T(1,128)S(1)} %add.14), channel_id=1, source_target_pairs={{0,4},{1,5},{2,6},{3,7},{4,0},{5,1},{6,2},{7,3},{8,12},{9,13},{10,... | collective-permute-start | bytes 3080 | tf_op jit(solution)/shard_map/ppermute | solution.py:217
  17.3 3.8 %collective-permute-start.3 = (f32[1,256]{1,0:T(1,128)S(1)}, f32[1,256]{1,0:T(1,128)S(1)}, u32[]{:S(2)}, u32[]{:S(2)}) collective-permute-start(f32[1,256]{1,0:T(1,128)S(1)} %add.15), channel_id=1, source_target_pairs={{0,8},{1,9},{2,10},{3,11},{4,12},{5,13},{6,14},{7,15},{8,0},{9,1},... | collective-permute-start | bytes 3080 | tf_op jit(solution)/shard_map/ppermute | solution.py:217
  21.1 5.3 %copy-start.9 = (f32[384]{0:T(512)S(1)}, f32[384]{0:T(512)}, u32[]{:S(2)}) copy-start(f32[384]{0:T(512)} %param.15) | copy-start | bytes 4612
  21.1 7.2 %copy-start.10 = (f32[384]{0:T(512)S(1)}, f32[384]{0:T(512)}, u32[]{:S(2)}) copy-start(f32[384]{0:T(512)} %param.14) | copy-start | bytes 4612
  21.1 7.2 %copy-start.11 = (f32[384]{0:T(512)S(1)}, f32[384]{0:T(512)}, u32[]{:S(2)}) copy-start(f32[384]{0:T(512)} %param.16) | copy-start | bytes 4612
  21.1 7.6 %copy-start.12 = (f32[3]{0:T(128)S(1)}, f32[3]{0:T(128)}, u32[]{:S(2)}) copy-start(f32[3]{0:T(128)} %constant.35) | copy-start | bytes 40
  21.2 5.2 %copy-start.5 = (f32[1,384,1536]{2,1,0:T(8,128)}, f32[1,384,1536]{2,1,0:T(8,128)S(1)}, u32[]{:S(2)}) copy-start(f32[1,384,1536]{2,1,0:T(8,128)S(1)} %collective-permute-done.4.q_near) | copy-start | bytes 7077892
  22.5 77.7 %collective-permute-start.6 = (f32[1,288,1536]{2,1,0:T(8,128)}, f32[1,288,1536]{2,1,0:T(8,128)}, u32[]{:S(2)}, u32[]{:S(2)}) collective-permute-start(f32[1,288,1536]{2,1,0:T(8,128)} %slice.27), channel_id=1, source_target_pairs={{0,15},{1,2},{2,1},{3,4},{4,3},{5,6},{6,5},{7,8},{8,7},{9,10},{10,... | collective-permute-start | bytes 5308424 | tf_op jit(solution)/shard_map/ppermute | solution.py:225
  26.4 80.0 %collective-permute-start.7 = (f32[1,96,1536]{2,1,0:T(8,128)}, f32[1,96,1536]{2,1,0:T(8,128)S(1)}, u32[]{:S(2)}, u32[]{:S(2)}) collective-permute-start(f32[1,96,1536]{2,1,0:T(8,128)} %slice.28), channel_id=1, source_target_pairs={{0,15},{1,2},{2,1},{3,4},{4,3},{5,6},{6,5},{7,8},{8,7},{9,10},{10,... | collective-permute-start | bytes 1769480 | tf_op jit(solution)/shard_map/ppermute | solution.py:225
  31.3 74.5 %collective-permute-start.8 = (f32[1,256]{1,0:T(1,128)S(1)}, f32[1,256]{1,0:T(1,128)S(1)}, u32[]{:S(2)}, u32[]{:S(2)}) collective-permute-start(f32[1,256]{1,0:T(1,128)S(1)} %add.16.mine), channel_id=1, source_target_pairs={{0,2},{1,3},{2,0},{3,1},{4,6},{5,7},{6,4},{7,5},{8,10},{9,11},{10,... | collective-permute-start | bytes 3080 | tf_op jit(solution)/shard_map/ppermute | solution.py:221
  48.5 1.7 %copy-start.2 = (f32[1,384,1536]{2,1,0:T(8,128)S(1)}, f32[1,384,1536]{2,1,0:T(8,128)}, u32[]{:S(2)}) copy-start(f32[1,384,1536]{2,1,0:T(8,128)} %c_down.1) | copy-start | bytes 7077892
  50.1 1.7 %copy-start.4 = (f32[1,384,1536]{2,1,0:T(8,128)S(1)}, f32[1,384,1536]{2,1,0:T(8,128)}, u32[]{:S(2)}) copy-start(f32[1,384,1536]{2,1,0:T(8,128)} %copy-done.3) | copy-start | bytes 7077892
  51.8 1.7 %copy-start.6 = (f32[1,384,1536]{2,1,0:T(8,128)S(1)}, f32[1,384,1536]{2,1,0:T(8,128)}, u32[]{:S(2)}) copy-start(f32[1,384,1536]{2,1,0:T(8,128)} %copy-done.5) | copy-start | bytes 7077892

commit v4 on v3

--- a/solution.py
+++ b/solution.py
@@ -10,8 +10,8 @@
 time_step = 0.6
 dissipation = 2.0
 
-STATE_PARTS = 4
-STATE_CUTS = (0, 3, 4)
+STATE_PARTS = 16
+STATE_CUTS = (0, 12, 15, 16)
 LOCAL_ROWS = 64
 ADD_ROWS = 96
 SUB = 8
@@ -163,7 +163,7 @@
 
 def add_rows(body, scal, base, part, whole, coef, start, small=()):
     rows, width = part.shape[1:]
-    block = math.gcd(ADD_ROWS, rows)
+    block = rows if rows <= ADD_ROWS else math.gcd(ADD_ROWS, rows)
     first = start // block
     full = pl.BlockSpec((1, block, width), lambda i: (0, first + i, 0))
     piece = pl.BlockSpec((1, block, width), lambda i: (0, i, 0))
@@ -218,7 +218,7 @@
         late, binned, state_near_rows = lax.optimization_barrier(
             (checkpoint, binned, state_near_rows)
         )
-        other = lax.ppermute(binned, "ax", [(i, i ^ 2) for i in range(count)])
+        other = lax.ppermute(binned, "ax", [(i, i ^ 3) for i in range(count)])
 
     edges = [rows * n // STATE_PARTS for n in STATE_CUTS]
     state_far_rows = [

time: 110 us -> 109 us (level)
  starting transfers between devices: 28.5 us -> 13.2 us
  waiting for transfers between devices: 43.6 us -> 57 us
  Pallas kernels: 19.2 us -> 20.7 us
    ppermute x1, starting transfers between devices: 17.2 us -> 0.02 us  [local(): other = lax.ppermute(binned, 'ax', [(i, i ^ 3) for i in range(count)])]
    ppermute x1, waiting for transfers between devices: 21.7 us -> 36.7 us  [local(): cot_far_rows = lax.ppermute(cotangent, 'ax', far)]
    ppermute x2 -> x3, starting transfers between devices: 2.99 us -> 4.8 us  [local(): lax.ppermute(late[:, low:high], 'ax', far)]
    pallas_call x3 -> x4, Pallas kernels: 10.9 us -> 12.4 us  [add_rows(): pl.pallas_call(body, grid=(rows // block,), out_shape=(shape, jax.ShapeDt...]
    ppermute x1, waiting for transfers between devices: 1.38 us -> 0.01 us  [local(): other = lax.ppermute(binned, 'ax', [(i, i ^ 3) for i in range(count)])]
    ppermute x2 -> x3, waiting for transfers between devices: 15 us -> 14.8 us  [local(): lax.ppermute(late[:, low:high], 'ax', far)]
    slice x2 -> x3, local copies, waits for them, and re-layouts: 2.2 us -> 2.24 us  [local(): late[:, low:high]]
  transfers between devices with their start and end apart: 9 -> 10, of which waited for: 8 -> 7; matrix products, arithmetic and copies ran while one was open for 5% -> 5% of each run, Pallas kernels for 16% -> 18%
where the time goes in v4:
time: 109 us; the launch traced here: 108 us
  waiting for transfers between devices  57 us (52%)
  Pallas kernels  20.7 us (19%)
  starting transfers between devices  13.2 us (12%)
  local copies, waits for them, and re-layouts  12.7 us (12%)
  between operations  2.71 us (2%)
  other arithmetic  2.18 us (2%)
    ppermute x1, waiting for transfers between devices, local(): cot_far_rows = lax.ppermute(cotangent, 'ax', far)  36.7 us
    ppermute x3, waiting for transfers between devices, local(): lax.ppermute(late[:, low:high], 'ax', far)  14.8 us
    pallas_call x4, Pallas kernels, add_rows(): pl.pallas_call(body, grid=(rows // block,), out_shape=(shape, jax.ShapeDt...  12.4 us
    unnamed x26, local copies, waits for them, and re-layouts  9.47 us
    pallas_call x1, Pallas kernels, local_parts(): pl.pallas_call(local_kernel, grid=(rows // block,), out_shape=(shape, sha...  6.09 us
    ppermute x3, starting transfers between devices, local(): lax.ppermute(binned, 'ax', [(i, i ^ n) for i in range(count)])  5.19 us
    ppermute x3, starting transfers between devices, local(): lax.ppermute(late[:, low:high], 'ax', far)  4.8 us
    ppermute x3, waiting for transfers between devices, local(): lax.ppermute(binned, 'ax', [(i, i ^ n) for i in range(count)])  3.87 us
  transfers between devices with their start and end apart: 10, of which 7 were waited for; matrix products, arithmetic and copies ran while one was open for 5% of the time, Pallas kernels for 18%

profile of v4, /device:TPU:1, one launch (start us, length us, event | category | flops | bytes accessed | tf_op | source)
XLA Modules:
  0.0 108.5 jit_solution(19735739206137783)
XLA Ops:
  0.6 0.1 collective-permute-start
  0.8 0.5 collective-permute-start.4
  1.2 2.6 %collective-permute-start.5 = (f32[1,384,1536]{2,1,0:T(8,128)}, f32[1,384,1536]{2,1,0:T(8,128)}, u32[]{:S(2)}, u32[]{:S(2)}) collective-permute-start(f32[1,384,1536]{2,1,0:T(8,128)} %c_down.1), channel_id=1, source_target_pairs={{0,15},{1,2},{2,1},{3,4},{4,3},{5,6},{6,5},{7,8},{8,7},{9,10},{10,... | collective-permute-start | bytes 7077896 | tf_op jit(solution)/shard_map/ppermute | solution.py:204
  3.8 1.6 %collective-permute-done.c_near = f32[1,384,1536]{2,1,0:T(8,128)S(1)} collective-permute-done((f32[1,384,1536]{2,1,0:T(8,128)}, f32[1,384,1536]{2,1,0:T(8,128)S(1)}, u32[]{:S(2)}, u32[]{:S(2)}) %collective-permute-start) | collective-permute-done | bytes 2359328 | tf_op jit(solution)/shard_map/ppermute | solution.py:205
  5.5 1.4 %copy-done.3 = f32[1,384,1536]{2,1,0:T(8,128)} copy-done((f32[1,384,1536]{2,1,0:T(8,128)}, f32[1,384,1536]{2,1,0:T(8,128)S(1)}, u32[]{:S(2)}) %copy-start.3) | copy-done | bytes 2359320
  6.9 1.7 %copy-done.1 = f32[1,384,1536]{2,1,0:T(8,128)S(1)} copy-done((f32[1,384,1536]{2,1,0:T(8,128)S(1)}, f32[1,384,1536]{2,1,0:T(8,128)}, u32[]{:S(2)}) %copy-start.1) | copy-done | bytes 2359320
  8.5 0.7 copy-done.7
  9.2 0.7 copy-done.8
  9.9 2.2 %shard_map.112 = (f32[1,1536]{1,0:T(1,128)S(1)}, f32[1,256]{1,0:T(1,128)S(1)}) custom-call(s32[1,1536]{1,0:T(1,128)S(1)} %copy-done.7, f32[1,256]{1,0:T(1,128)S(1)} %bitcast.9, f32[1,384,1536]{2,1,0:T(8,128)S(1)} %copy-done.1), custom_call_target="tpu_custom_call" | custom-call | tf_op jit(solution)/shard_map/pallas_call | solution.py:58
  12.1 0.0 copy-start.10
  12.1 0.0 copy-start.11
  12.1 0.0 copy-start.12
  12.1 1.6 %collective-permute-start.1 = (f32[1,256]{1,0:T(1,128)S(1)}, f32[1,256]{1,0:T(1,128)S(1)}, u32[]{:S(2)}, u32[]{:S(2)}) collective-permute-start(f32[1,256]{1,0:T(1,128)S(1)} %get-tuple-element.17), channel_id=1, source_target_pairs={{0,1},{1,0},{2,3},{3,2},{4,5},{5,4},{6,7},{7,6},{8,9},{9,8},{10,11... | collective-permute-start | bytes 3080 | tf_op jit(solution)/shard_map/ppermute | solution.py:217
  13.7 0.8 collective-permute-done.1
  14.5 1.3 %collective-permute-start.2 = (f32[1,256]{1,0:T(1,128)S(1)}, f32[1,256]{1,0:T(1,128)S(1)}, u32[]{:S(2)}, u32[]{:S(2)}) collective-permute-start(f32[1,256]{1,0:T(1,128)S(1)} %add.14), channel_id=1, source_target_pairs={{0,4},{1,5},{2,6},{3,7},{4,0},{5,1},{6,2},{7,3},{8,12},{9,13},{10,... | collective-permute-start | bytes 3080 | tf_op jit(solution)/shard_map/ppermute | solution.py:217
  15.8 1.6 %collective-permute-done.2 = f32[1,256]{1,0:T(1,128)S(1)} collective-permute-done((f32[1,256]{1,0:T(1,128)S(1)}, f32[1,256]{1,0:T(1,128)S(1)}, u32[]{:S(2)}, u32[]{:S(2)}) %collective-permute-start.2) | collective-permute-done | bytes 1056 | tf_op jit(solution)/shard_map/ppermute | solution.py:217
  17.4 2.3 %collective-permute-start.3 = (f32[1,256]{1,0:T(1,128)S(1)}, f32[1,256]{1,0:T(1,128)S(1)}, u32[]{:S(2)}, u32[]{:S(2)}) collective-permute-start(f32[1,256]{1,0:T(1,128)S(1)} %add.15), channel_id=1, source_target_pairs={{0,8},{1,9},{2,10},{3,11},{4,12},{5,13},{6,14},{7,15},{8,0},{9,1},... | collective-permute-start | bytes 3080 | tf_op jit(solution)/shard_map/ppermute | solution.py:217
  19.7 1.5 %collective-permute-done.3 = f32[1,256]{1,0:T(1,128)S(1)} collective-permute-done((f32[1,256]{1,0:T(1,128)S(1)}, f32[1,256]{1,0:T(1,128)S(1)}, u32[]{:S(2)}, u32[]{:S(2)}) %collective-permute-start.3) | collective-permute-done | bytes 1056 | tf_op jit(solution)/shard_map/ppermute | solution.py:217
  21.2 0.0 collective-permute-done.4.q_near
  21.2 0.0 copy-start.5
  21.2 1.4 %slice.30 = f32[1,288,1536]{2,1,0:T(8,128)} slice(f32[1,384,1536]{2,1,0:T(8,128)S(1)} %copy-done), slice={[0:1], [0:288], [0:1536]} | slice | bytes 3538944 | tf_op jit(solution)/shard_map/slice | solution.py:225
  22.7 3.0 %collective-permute-start.6 = (f32[1,288,1536]{2,1,0:T(8,128)}, f32[1,288,1536]{2,1,0:T(8,128)}, u32[]{:S(2)}, u32[]{:S(2)}) collective-permute-start(f32[1,288,1536]{2,1,0:T(8,128)} %slice.30), channel_id=1, source_target_pairs={{0,15},{1,2},{2,1},{3,4},{4,3},{5,6},{6,5},{7,8},{8,7},{9,10},{10,... | collective-permute-start | bytes 5308424 | tf_op jit(solution)/shard_map/ppermute | solution.py:225
  25.7 0.6 slice.26
  26.3 0.1 slice.28
  27.0 0.7 fusion
  27.7 0.8 slice.31
  28.5 0.0 collective-permute-start.7
  28.5 0.6 pad_maximum_fusion.1
  29.2 1.8 %collective-permute-start.8 = (f32[1,24,1536]{2,1,0:T(8,128)S(1)}, f32[1,24,1536]{2,1,0:T(8,128)S(1)}, u32[]{:S(2)}, u32[]{:S(2)}) collective-permute-start(f32[1,24,1536]{2,1,0:T(8,128)S(1)} %slice.32), channel_id=1, source_target_pairs={{0,15},{1,2},{2,1},{3,4},{4,3},{5,6},{6,5},{7,8},{8,7},{9,10},{10,... | collective-permute-start | bytes 442376 | tf_op jit(solution)/shard_map/ppermute | solution.py:225
  31.0 0.1 pad_maximum_fusion.2
  31.1 0.1 copy.24.coef
  31.3 0.1 copy.25.coef
  32.7 0.8 pad_maximum_fusion.3.scal
  33.5 0.0 collective-permute-start.9
  33.5 0.0 copy-start.2
  33.5 1.7 %copy-done.2 = f32[1,384,1536]{2,1,0:T(8,128)S(1)} copy-done((f32[1,384,1536]{2,1,0:T(8,128)S(1)}, f32[1,384,1536]{2,1,0:T(8,128)}, u32[]{:S(2)}) %copy-start.2) | copy-done | bytes 2359320
  35.2 1.7 %copy-done.4 = f32[1,384,1536]{2,1,0:T(8,128)S(1)} copy-done((f32[1,384,1536]{2,1,0:T(8,128)S(1)}, f32[1,384,1536]{2,1,0:T(8,128)}, u32[]{:S(2)}) %copy-start.4) | copy-done | bytes 2359320
  36.8 1.7 %copy-done.6 = f32[1,384,1536]{2,1,0:T(8,128)S(1)} copy-done((f32[1,384,1536]{2,1,0:T(8,128)S(1)}, f32[1,384,1536]{2,1,0:T(8,128)}, u32[]{:S(2)}) %copy-start.6) | copy-done | bytes 2359320
  38.5 6.1 %shard_map.113 = (f32[1,384,1536]{2,1,0:T(8,128)}, f32[1,384,1536]{2,1,0:T(8,128)}) custom-call(f32[3]{0:T(128)S(1)} %pad_maximum_fusion.3.scal, f32[1,384,1536]{2,1,0:T(8,128)S(1)} %copy-done, f32[1,384,1536]{2,1,0:T(8,128)S(1)} %copy-done, f32[1,384,1536]{2,1,0:T(8,128)S(1)} %copy-done, f32[1,384,1536]{2,1,0:T(8,128)S(1)} %copy-done.6, ...), custom_call_target="tpu_custom_call" | custom-call | flops 29491200 | bytes 14155776 | tf_op jit(solution)/shard_map/pallas_call | solution.py:132
  44.6 36.7 %collective-permute-done.5.far = f32[1,384,1536]{2,1,0:T(8,128)} collective-permute-done((f32[1,384,1536]{2,1,0:T(8,128)}, f32[1,384,1536]{2,1,0:T(8,128)}, u32[]{:S(2)}, u32[]{:S(2)}) %collective-permute-start.5) | collective-permute-done | bytes 2359328 | tf_op jit(solution)/shard_map/ppermute | solution.py:204
  81.2 4.6 %shard_map.114 = f32[1,384,1536]{2,1,0:T(8,128)} custom-call(f32[3]{0:T(128)S(1)} %pad_maximum_fusion.3.scal, f32[1,384,1536]{2,1,0:T(8,128)} %get-tuple-element.22.base, f32[1,384,1536]{2,1,0:T(8,128)} %collective-permute-done.5.far, f32[1,384,1536]{2,1,0:T(8,128)S(1)} %copy-done, f32[384,3]{1,0:T(8,128)S(1)} %copy.25.coef), custom_call_target="tpu_custom_call", output_to_operand_aliasing={{}: (1, {})} | custom-call | flops 5898240 | bytes 9437184 | tf_op jit(solution)/shard_map/pallas_call | solution.py:173
  85.8 14.4 %collective-permute-done.6.far = f32[1,288,1536]{2,1,0:T(8,128)} collective-permute-done((f32[1,288,1536]{2,1,0:T(8,128)}, f32[1,288,1536]{2,1,0:T(8,128)}, u32[]{:S(2)}, u32[]{:S(2)}) %collective-permute-start.6) | collective-permute-done | bytes 1769504 | tf_op jit(solution)/shard_map/ppermute | solution.py:225
  100.2 4.2 %shard_map.115.base = f32[1,384,1536]{2,1,0:T(8,128)} custom-call(f32[3]{0:T(128)S(1)} %pad_maximum_fusion.3.scal, f32[1,384,1536]{2,1,0:T(8,128)} %get-tuple-element.23.base, f32[1,288,1536]{2,1,0:T(8,128)} %collective-permute-done.6.far, f32[384,3]{1,0:T(8,128)S(1)} %copy.25.coef), custom_call_target="tpu_custom_call", output_to_operand_aliasing={{}: (1, {})} | custom-call | flops 4423680 | bytes 7077888 | tf_op jit(solution)/shard_map/pallas_call | solution.py:173
  104.4 0.4 collective-permute-done.7.far
  104.8 2.0 %shard_map.116.base = f32[1,384,1536]{2,1,0:T(8,128)} custom-call(f32[3]{0:T(128)S(1)} %pad_maximum_fusion.3.scal, f32[1,384,1536]{2,1,0:T(8,128)} %shard_map.115.base, f32[1,72,1536]{2,1,0:T(8,128)S(1)} %collective-permute-done.7.far, f32[384,3]{1,0:T(8,128)S(1)} %copy.25.coef), custom_call_target="tpu_custom_call", output_to_operand_aliasing={{}: (1, {})} | custom-call | flops 1105920 | bytes 1769472 | tf_op jit(solution)/shard_map/pallas_call | solution.py:173
  106.8 0.0 collective-permute-done.9.other
  106.8 0.0 collective-permute-done.8.far
  106.8 1.7 %shard_map.117 = (f32[1,384,1536]{2,1,0:T(8,128)}, f32[1,256]{1,0:T(1,128)}) custom-call(f32[3]{0:T(128)S(1)} %pad_maximum_fusion.3.scal, f32[1,384,1536]{2,1,0:T(8,128)} %shard_map.116.base, f32[1,24,1536]{2,1,0:T(8,128)S(1)} %collective-permute-done.8.far, f32[1,256]{1,0:T(1,128)S(1)} %add.16.mine, ...), custom_call_target="tpu_custom_call", output_to_operand_aliasing={{0}: (1, {})} | custom-call | flops 368640 | bytes 589824 | tf_op jit(solution)/shard_map/pallas_call | solution.py:173
  (26 shorter events, 0.1 us)
Async XLA Ops:
  0.6 20.6 %copy-start = (f32[1,384,1536]{2,1,0:T(8,128)S(1)}, f32[1,384,1536]{2,1,0:T(8,128)}, u32[]{:S(2)}) copy-start(f32[1,384,1536]{2,1,0:T(8,128)} %state.1) | copy-start | bytes 7077892
  0.6 4.8 %collective-permute-start = (f32[1,384,1536]{2,1,0:T(8,128)}, f32[1,384,1536]{2,1,0:T(8,128)S(1)}, u32[]{:S(2)}, u32[]{:S(2)}) collective-permute-start(f32[1,384,1536]{2,1,0:T(8,128)} %c_down.1), channel_id=1, source_target_pairs={{0,1},{1,0},{2,3},{3,2},{4,5},{5,4},{6,7},{7,6},{8,9},{9,8},{10,11... | collective-permute-start | bytes 7077896 | tf_op jit(solution)/shard_map/ppermute | solution.py:205
  0.8 20.5 %collective-permute-start.4 = (f32[1,384,1536]{2,1,0:T(8,128)}, f32[1,384,1536]{2,1,0:T(8,128)S(1)}, u32[]{:S(2)}, u32[]{:S(2)}) collective-permute-start(f32[1,384,1536]{2,1,0:T(8,128)} %state.1), channel_id=1, source_target_pairs={{0,1},{1,0},{2,3},{3,2},{4,5},{5,4},{6,7},{7,6},{8,9},{9,8},{10,11... | collective-permute-start | bytes 7077896 | tf_op jit(solution)/shard_map/ppermute | solution.py:206
  1.2 80.0 %collective-permute-start.5 = (f32[1,384,1536]{2,1,0:T(8,128)}, f32[1,384,1536]{2,1,0:T(8,128)}, u32[]{:S(2)}, u32[]{:S(2)}) collective-permute-start(f32[1,384,1536]{2,1,0:T(8,128)} %c_down.1), channel_id=1, source_target_pairs={{0,15},{1,2},{2,1},{3,4},{4,3},{5,6},{6,5},{7,8},{8,7},{9,10},{10,... | collective-permute-start | bytes 7077896 | tf_op jit(solution)/shard_map/ppermute | solution.py:204
  5.5 1.4 %copy-start.3 = (f32[1,384,1536]{2,1,0:T(8,128)}, f32[1,384,1536]{2,1,0:T(8,128)S(1)}, u32[]{:S(2)}) copy-start(f32[1,384,1536]{2,1,0:T(8,128)S(1)} %collective-permute-done.c_near) | copy-start | bytes 7077892
  6.9 1.7 %copy-start.1 = (f32[1,384,1536]{2,1,0:T(8,128)S(1)}, f32[1,384,1536]{2,1,0:T(8,128)}, u32[]{:S(2)}) copy-start(f32[1,384,1536]{2,1,0:T(8,128)} %c_down.1) | copy-start | bytes 7077892
  8.5 0.7 copy-start.7
  9.2 0.7 copy-start.8
  12.1 13.6 %copy-start.9 = (f32[384]{0:T(512)S(1)}, f32[384]{0:T(512)}, u32[]{:S(2)}) copy-start(f32[384]{0:T(512)} %param.15) | copy-start | bytes 4612
  12.1 14.9 %copy-start.10 = (f32[384]{0:T(512)S(1)}, f32[384]{0:T(512)}, u32[]{:S(2)}) copy-start(f32[384]{0:T(512)} %param.14) | copy-start | bytes 4612
  12.1 14.9 %copy-start.11 = (f32[384]{0:T(512)S(1)}, f32[384]{0:T(512)}, u32[]{:S(2)}) copy-start(f32[384]{0:T(512)} %param.16) | copy-start | bytes 4612
  12.1 14.9 %copy-start.12 = (f32[3]{0:T(128)S(1)}, f32[3]{0:T(128)}, u32[]{:S(2)}) copy-start(f32[3]{0:T(128)} %constant.35) | copy-start | bytes 40
  12.1 2.4 %collective-permute-start.1 = (f32[1,256]{1,0:T(1,128)S(1)}, f32[1,256]{1,0:T(1,128)S(1)}, u32[]{:S(2)}, u32[]{:S(2)}) collective-permute-start(f32[1,256]{1,0:T(1,128)S(1)} %get-tuple-element.17), channel_id=1, source_target_pairs={{0,1},{1,0},{2,3},{3,2},{4,5},{5,4},{6,7},{7,6},{8,9},{9,8},{10,11... | collective-permute-start | bytes 3080 | tf_op jit(solution)/shard_map/ppermute | solution.py:217
  14.5 2.9 %collective-permute-start.2 = (f32[1,256]{1,0:T(1,128)S(1)}, f32[1,256]{1,0:T(1,128)S(1)}, u32[]{:S(2)}, u32[]{:S(2)}) collective-permute-start(f32[1,256]{1,0:T(1,128)S(1)} %add.14), channel_id=1, source_target_pairs={{0,4},{1,5},{2,6},{3,7},{4,0},{5,1},{6,2},{7,3},{8,12},{9,13},{10,... | collective-permute-start | bytes 3080 | tf_op jit(solution)/shard_map/ppermute | solution.py:217
  17.4 3.8 %collective-permute-start.3 = (f32[1,256]{1,0:T(1,128)S(1)}, f32[1,256]{1,0:T(1,128)S(1)}, u32[]{:S(2)}, u32[]{:S(2)}) collective-permute-start(f32[1,256]{1,0:T(1,128)S(1)} %add.15), channel_id=1, source_target_pairs={{0,8},{1,9},{2,10},{3,11},{4,12},{5,13},{6,14},{7,15},{8,0},{9,1},... | collective-permute-start | bytes 3080 | tf_op jit(solution)/shard_map/ppermute | solution.py:217
  21.2 8.0 %copy-start.5 = (f32[1,384,1536]{2,1,0:T(8,128)}, f32[1,384,1536]{2,1,0:T(8,128)S(1)}, u32[]{:S(2)}) copy-start(f32[1,384,1536]{2,1,0:T(8,128)S(1)} %collective-permute-done.4.q_near) | copy-start | bytes 7077892
  22.7 77.5 %collective-permute-start.6 = (f32[1,288,1536]{2,1,0:T(8,128)}, f32[1,288,1536]{2,1,0:T(8,128)}, u32[]{:S(2)}, u32[]{:S(2)}) collective-permute-start(f32[1,288,1536]{2,1,0:T(8,128)} %slice.30), channel_id=1, source_target_pairs={{0,15},{1,2},{2,1},{3,4},{4,3},{5,6},{6,5},{7,8},{8,7},{9,10},{10,... | collective-permute-start | bytes 5308424 | tf_op jit(solution)/shard_map/ppermute | solution.py:225
  28.5 76.3 %collective-permute-start.7 = (f32[1,72,1536]{2,1,0:T(8,128)}, f32[1,72,1536]{2,1,0:T(8,128)S(1)}, u32[]{:S(2)}, u32[]{:S(2)}) collective-permute-start(f32[1,72,1536]{2,1,0:T(8,128)} %slice.31), channel_id=1, source_target_pairs={{0,15},{1,2},{2,1},{3,4},{4,3},{5,6},{6,5},{7,8},{8,7},{9,10},{10,... | collective-permute-start | bytes 1327112 | tf_op jit(solution)/shard_map/ppermute | solution.py:225
  29.2 77.6 %collective-permute-start.8 = (f32[1,24,1536]{2,1,0:T(8,128)S(1)}, f32[1,24,1536]{2,1,0:T(8,128)S(1)}, u32[]{:S(2)}, u32[]{:S(2)}) collective-permute-start(f32[1,24,1536]{2,1,0:T(8,128)S(1)} %slice.32), channel_id=1, source_target_pairs={{0,15},{1,2},{2,1},{3,4},{4,3},{5,6},{6,5},{7,8},{8,7},{9,10},{10,... | collective-permute-start | bytes 442376 | tf_op jit(solution)/shard_map/ppermute | solution.py:225
  33.5 73.3 %collective-permute-start.9 = (f32[1,256]{1,0:T(1,128)S(1)}, f32[1,256]{1,0:T(1,128)S(1)}, u32[]{:S(2)}, u32[]{:S(2)}) collective-permute-start(f32[1,256]{1,0:T(1,128)S(1)} %add.16.mine), channel_id=1, source_target_pairs={{0,3},{1,2},{2,1},{3,0},{4,7},{5,6},{6,5},{7,4},{8,11},{9,10},{10,... | collective-permute-start | bytes 3080 | tf_op jit(solution)/shard_map/ppermute | solution.py:221
  33.5 1.7 %copy-start.2 = (f32[1,384,1536]{2,1,0:T(8,128)S(1)}, f32[1,384,1536]{2,1,0:T(8,128)}, u32[]{:S(2)}) copy-start(f32[1,384,1536]{2,1,0:T(8,128)} %c_down.1) | copy-start | bytes 7077892
  35.2 1.7 %copy-start.4 = (f32[1,384,1536]{2,1,0:T(8,128)S(1)}, f32[1,384,1536]{2,1,0:T(8,128)}, u32[]{:S(2)}) copy-start(f32[1,384,1536]{2,1,0:T(8,128)} %copy-done.3) | copy-start | bytes 7077892
  36.8 1.7 %copy-start.6 = (f32[1,384,1536]{2,1,0:T(8,128)S(1)}, f32[1,384,1536]{2,1,0:T(8,128)}, u32[]{:S(2)}) copy-start(f32[1,384,1536]{2,1,0:T(8,128)} %copy-done.5) | copy-start | bytes 7077892

commit v5 on v4

--- a/solution.py
+++ b/solution.py
@@ -151,40 +151,32 @@
     out[0] = base[0] + step * (x + (0.5 * side) * (x * (coef[:, 0:1] + 0.5 * x)))
 
 
-def state_last(scal, base, far, mine, other, coef, out, gradient):
-    state_far(scal, base, far, coef, out)
-    gradient[...] = scal[2] * (mine[...] + other[...])
-
-
 def cot_far(scal, base, far, state, coef, out):
     step, side = scal[0], scal[1]
     out[0] = base[0] + step * far[0] * (1.0 - (0.5 * side) * (coef[:, 0:1] + state[0]))
 
 
-def add_rows(body, scal, base, part, whole, coef, start, small=()):
+def add_rows(body, scal, base, part, whole, coef, start):
     rows, width = part.shape[1:]
     block = rows if rows <= ADD_ROWS else math.gcd(ADD_ROWS, rows)
     first = start // block
     full = pl.BlockSpec((1, block, width), lambda i: (0, first + i, 0))
     piece = pl.BlockSpec((1, block, width), lambda i: (0, i, 0))
     column = pl.BlockSpec((block, coef.shape[1]), lambda i: (first + i, 0))
-    short = [pl.BlockSpec(x.shape, lambda i: (0, 0)) for x in small]
-    shape = jax.ShapeDtypeStruct(base.shape, base.dtype)
     return pl.pallas_call(
         body,
         grid=(rows // block,),
-        out_shape=(shape, jax.ShapeDtypeStruct(small[0].shape, base.dtype)) if small else shape,
+        out_shape=jax.ShapeDtypeStruct(base.shape, base.dtype),
         in_specs=[pl.BlockSpec(memory_space=pltpu.SMEM), full, piece]
-        + short
         + [full] * len(whole)
         + [column],
-        out_specs=(full, short[0]) if small else full,
+        out_specs=full,
         input_output_aliases={1: 0},
         compiler_params=pltpu.CompilerParams(vmem_limit_bytes=40 << 20),
         cost_estimate=pl.CostEstimate(
             flops=10 * rows * width, bytes_accessed=4 * rows * width * 4, transcendentals=0
         ),
-    )(scal, base, part, *small, *whole, coef)
+    )(scal, base, part, *whole, coef)
 
 
 def local(
@@ -205,20 +197,20 @@
     cot_near_rows = lax.ppermute(cotangent, "ax", near)
     state_near_rows = lax.ppermute(checkpoint, "ax", near)
 
-    cot_now, cot_near_rows = lax.optimization_barrier((cotangent, cot_near_rows))
-    wall, binned = wall_and_bins(patch_ids, amplitudes, cot_now)
-
+    wall, binned = wall_and_bins(patch_ids, amplitudes, cotangent)
+
+    late, state_near_rows = lax.optimization_barrier((checkpoint, state_near_rows))
     if count & (count - 1) or count < 4:
         binned = lax.psum(binned, "ax")
-        other = jnp.zeros_like(binned)
-        late = checkpoint
     else:
         for n in [1] + [1 << n for n in range(2, count.bit_length() - 1)]:
             binned = binned + lax.ppermute(binned, "ax", [(i, i ^ n) for i in range(count)])
-        late, binned, state_near_rows = lax.optimization_barrier(
-            (checkpoint, binned, state_near_rows)
-        )
-        other = lax.ppermute(binned, "ax", [(i, i ^ 3) for i in range(count)])
+        lead = [i for i in range(count) if i % 4 in (0, 3)]
+        other = lax.ppermute(binned, "ax", [(i, i ^ 3) for i in lead])
+        whole = binned + other
+        given = lax.ppermute(whole, "ax", [(i, i ^ 1) for i in lead])
+        place = lax.axis_index("ax") % 4
+        binned = jnp.where((place == 0) | (place == 3), whole, given)
 
     edges = [rows * n // STATE_PARTS for n in STATE_CUTS]
     state_far_rows = [
@@ -229,7 +221,8 @@
     side = 1.0 - 2.0 * (lax.axis_index("ax") % 2).astype(jnp.float32)
     total_cells = checkpoint.shape[0] * count * checkpoint.shape[2]
     norm_factor = (patches / total_cells) ** 0.5
-    scal = jnp.stack([step_size, side, step_size * radial_diffusion[-1] * norm_factor])
+    gradient = (step_size * radial_diffusion[-1] * norm_factor) * binned[0]
+    scal = jnp.stack([step_size, side])
     coef = jnp.stack([axial_speed, radial_diffusion, azimuth_diffusion], axis=1)
 
     advanced, adjoint = local_parts(
@@ -239,10 +232,13 @@
     advanced, adjoint = lax.optimization_barrier((advanced, adjoint))
     for low, part in zip(edges[:-2], state_far_rows[:-1]):
         advanced = add_rows(state_far, scal, advanced, part, [], coef, low)
-    advanced, gradient = add_rows(
-        state_last, scal, advanced, state_far_rows[-1], [], coef, edges[-2], (binned, other)
-    )
-    return (advanced, adjoint, gradient[0])
+    advanced, gradient = lax.optimization_barrier((advanced, gradient))
+    low, x = edges[-2], state_far_rows[-1]
+    last = advanced[:, low:] + step_size * (
+        x + (0.5 * side) * (x * (axial_speed[None, low:, None] + 0.5 * x))
+    )
+    advanced = lax.dynamic_update_slice(advanced, last, (0, low, 0))
+    return (advanced, adjoint, gradient)
 
 
 def solution(mesh):

time: 109 us -> 110 us (level)
  other arithmetic: 2.18 us -> 4.84 us
  starting transfers between devices: 13.2 us -> 11.4 us
  waiting for transfers between devices: 57 us -> 58.7 us
  local copies, waits for them, and re-layouts: 12.7 us -> 11.2 us
    ppermute x1, waiting for transfers between devices: 36.7 us -> 5.47 us  [local(): cot_far_rows = lax.ppermute(cotangent, 'ax', far)]
    ppermute x1 -> x2, waiting for transfers between devices: 0.01 us -> 28.5 us  [the longest x1 28.5 us: local(): given = lax.ppermute(whole, 'ax', [(i, i ^ 1) for i in lead])]
    ppermute x1, waiting for transfers between devices: 0.01 us -> 4.22 us  [local(): state_near_rows = lax.ppermute(checkpoint, 'ax', near)]
    unnamed x26 -> x22, local copies, waits for them, and re-layouts: 9.47 us -> 6.43 us
    dynamic_update_slice x0 -> x1, other arithmetic: none -> 2.23 us  [local(): advanced = lax.dynamic_update_slice(advanced, last, (0, low, 0))]
    ppermute x3, starting transfers between devices: 5.19 us -> 3.26 us  [local(): lax.ppermute(binned, 'ax', [(i, i ^ n) for i in range(count)])]
    ppermute x1 -> x2, starting transfers between devices: 0.02 us -> 1.93 us  [the longest x1 1.28 us: local(): given = lax.ppermute(whole, 'ax', [(i, i ^ 1) for i in lead])]
    ppermute x3, waiting for transfers between devices: 3.87 us -> 5.72 us  [local(): lax.ppermute(binned, 'ax', [(i, i ^ n) for i in range(count)])]
  transfers between devices with their start and end apart: 10 -> 11, of which waited for: 7 -> 7; matrix products, arithmetic and copies ran while one was open for 5% -> 7% of each run, Pallas kernels for 18% -> 18%
where the time goes in v5:
time: 110 us; the launch traced here: 109 us
  waiting for transfers between devices  58.7 us (53%)
  Pallas kernels  20.2 us (18%)
  starting transfers between devices  11.4 us (10%)
  local copies, waits for them, and re-layouts  11.2 us (10%)
  other arithmetic  4.84 us (4%)
  between operations  2.71 us (2%)
    ppermute x1, waiting for transfers between devices, local(): given = lax.ppermute(whole, 'ax', [(i, i ^ 1) for i in lead])  28.5 us
    ppermute x3, waiting for transfers between devices, local(): lax.ppermute(late[:, low:high], 'ax', far)  14.8 us
    pallas_call x3, Pallas kernels, add_rows(): pl.pallas_call(body, grid=(rows // block,), out_shape=jax.ShapeDtypeStruc...  10.7 us
    pallas_call x1, Pallas kernels, local_parts(): pl.pallas_call(local_kernel, grid=(rows // block,), out_shape=(shape, sha...  7.25 us
    unnamed x22, local copies, waits for them, and re-layouts  6.43 us
    ppermute x3, waiting for transfers between devices, local(): lax.ppermute(binned, 'ax', [(i, i ^ n) for i in range(count)])  5.72 us
    ppermute x1, waiting for transfers between devices, local(): cot_far_rows = lax.ppermute(cotangent, 'ax', far)  5.47 us
    ppermute x1, waiting for transfers between devices, local(): state_near_rows = lax.ppermute(checkpoint, 'ax', near)  4.22 us
  transfers between devices with their start and end apart: 11, of which 7 were waited for; matrix products, arithmetic and copies ran while one was open for 7% of the time, Pallas kernels for 18%

profile of v5, /device:TPU:1, one launch (start us, length us, event | category | flops | bytes accessed | tf_op | source)
XLA Modules:
  0.0 109.1 jit_solution(6575700641060622566)
XLA Ops:
  0.6 0.0 copy-start.10
  0.6 0.0 copy-start
  0.7 0.1 collective-permute-start
  0.8 0.5 collective-permute-start.1
  1.3 2.6 %collective-permute-start.2 = (f32[1,384,1536]{2,1,0:T(8,128)}, f32[1,384,1536]{2,1,0:T(8,128)}, u32[]{:S(2)}, u32[]{:S(2)}) collective-permute-start(f32[1,384,1536]{2,1,0:T(8,128)} %c_down.1), channel_id=1, source_target_pairs={{0,15},{1,2},{2,1},{3,4},{4,3},{5,6},{6,5},{7,8},{8,7},{9,10},{10,... | collective-permute-start | bytes 7077896 | tf_op jit(solution)/shard_map/ppermute | solution.py:196
  3.9 4.2 %collective-permute-done.q_near = f32[1,384,1536]{2,1,0:T(8,128)S(1)} collective-permute-done((f32[1,384,1536]{2,1,0:T(8,128)}, f32[1,384,1536]{2,1,0:T(8,128)S(1)}, u32[]{:S(2)}, u32[]{:S(2)}) %collective-permute-start) | collective-permute-done | bytes 2359328 | tf_op jit(solution)/shard_map/ppermute | solution.py:198
  8.1 1.4 %copy-done.3 = f32[1,384,1536]{2,1,0:T(8,128)} copy-done((f32[1,384,1536]{2,1,0:T(8,128)}, f32[1,384,1536]{2,1,0:T(8,128)S(1)}, u32[]{:S(2)}) %copy-start.3) | copy-done | bytes 2359320
  9.5 2.9 %slice.36 = f32[1,288,1536]{2,1,0:T(8,128)} slice(f32[1,384,1536]{2,1,0:T(8,128)} %state.1), slice={[0:1], [0:288], [0:1536]} | slice | bytes 3538944 | tf_op jit(solution)/shard_map/slice | solution.py:217
  12.4 2.6 %collective-permute-start.3 = (f32[1,288,1536]{2,1,0:T(8,128)}, f32[1,288,1536]{2,1,0:T(8,128)}, u32[]{:S(2)}, u32[]{:S(2)}) collective-permute-start(f32[1,288,1536]{2,1,0:T(8,128)} %slice.36), channel_id=1, source_target_pairs={{0,15},{1,2},{2,1},{3,4},{4,3},{5,6},{6,5},{7,8},{8,7},{9,10},{10,... | collective-permute-start | bytes 5308424 | tf_op jit(solution)/shard_map/ppermute | solution.py:217
  15.0 0.0 copy-done.6
  15.0 1.7 %copy-done.1 = f32[1,384,1536]{2,1,0:T(8,128)S(1)} copy-done((f32[1,384,1536]{2,1,0:T(8,128)S(1)}, f32[1,384,1536]{2,1,0:T(8,128)}, u32[]{:S(2)}) %copy-start.1) | copy-done | bytes 2359320
  16.7 2.2 %shard_map.112 = (f32[1,1536]{1,0:T(1,128)S(1)}, f32[1,256]{1,0:T(1,128)S(1)}) custom-call(s32[1,1536]{1,0:T(1,128)S(1)} %copy-done.5, f32[1,256]{1,0:T(1,128)S(1)} %bitcast.8, f32[1,384,1536]{2,1,0:T(8,128)S(1)} %copy-done.1), custom_call_target="tpu_custom_call" | custom-call | tf_op jit(solution)/shard_map/pallas_call | solution.py:58
  18.9 3.2 %collective-permute-start.5 = (f32[1,256]{1,0:T(1,128)S(1)}, f32[1,256]{1,0:T(1,128)S(1)}, u32[]{:S(2)}, u32[]{:S(2)}) collective-permute-start(f32[1,256]{1,0:T(1,128)S(1)} %get-tuple-element.19), channel_id=1, source_target_pairs={{0,1},{1,0},{2,3},{3,2},{4,5},{5,4},{6,7},{7,6},{8,9},{9,8},{10,11... | collective-permute-start | bytes 3080 | tf_op jit(solution)/shard_map/ppermute | solution.py:207
  22.1 0.6 slice.32
  23.3 0.0 copy-done.10
  23.3 0.6 fusion.1
  23.9 0.7 pad_maximum_fusion.1
  24.7 0.1 slice.34
  24.7 0.0 collective-permute-done.5
  24.8 0.1 collective-permute-start.6
  24.8 0.8 slice.37
  25.7 0.0 collective-permute-start.4
  25.7 0.1 pad_maximum_fusion.2
  25.8 1.9 %collective-permute-done.6 = f32[1,256]{1,0:T(1,128)S(1)} collective-permute-done((f32[1,256]{1,0:T(1,128)S(1)}, f32[1,256]{1,0:T(1,128)S(1)}, u32[]{:S(2)}, u32[]{:S(2)}) %collective-permute-start.6) | collective-permute-done | bytes 1056 | tf_op jit(solution)/shard_map/ppermute | solution.py:207
  27.7 0.0 collective-permute-start.7
  27.7 3.8 %collective-permute-done.7 = f32[1,256]{1,0:T(1,128)S(1)} collective-permute-done((f32[1,256]{1,0:T(1,128)S(1)}, f32[1,256]{1,0:T(1,128)S(1)}, u32[]{:S(2)}, u32[]{:S(2)}) %collective-permute-start.7) | collective-permute-done | bytes 1056 | tf_op jit(solution)/shard_map/ppermute | solution.py:207
  31.5 0.7 collective-permute-start.8
  32.2 0.6 pad_maximum_fusion.3.scal
  32.8 0.0 collective-permute-done.8
  32.8 1.3 %collective-permute-start.9 = (f32[1,256]{1,0:T(1,128)S(1)}, f32[1,256]{1,0:T(1,128)S(1)}, u32[]{:S(2)}, u32[]{:S(2)}) collective-permute-start(f32[1,256]{1,0:T(1,128)S(1)} %add.38), channel_id=1, source_target_pairs={{0,1},{3,2},{4,5},{7,6},{8,9},{11,10},{12,13},{15,14},{16,17},{19,... | collective-permute-start | bytes 3080 | tf_op jit(solution)/shard_map/ppermute | solution.py:211
  34.1 0.1 slice.40
  34.2 0.1 copy.23.coef
  34.4 0.1 copy.24.coef
  35.8 28.5 %collective-permute-done.9 = f32[1,256]{1,0:T(1,128)S(1)} collective-permute-done((f32[1,256]{1,0:T(1,128)S(1)}, f32[1,256]{1,0:T(1,128)S(1)}, u32[]{:S(2)}, u32[]{:S(2)}) %collective-permute-start.9) | collective-permute-done | bytes 1056 | tf_op jit(solution)/shard_map/ppermute | solution.py:211
  64.3 0.4 collective-permute-start.10
  64.7 0.6 fusion
  65.2 0.0 collective-permute-done.1.c_near
  65.2 1.7 %copy-done.2 = f32[1,384,1536]{2,1,0:T(8,128)S(1)} copy-done((f32[1,384,1536]{2,1,0:T(8,128)S(1)}, f32[1,384,1536]{2,1,0:T(8,128)}, u32[]{:S(2)}) %copy-start.2) | copy-done | bytes 2359320
  66.9 1.7 %copy-done.4 = f32[1,384,1536]{2,1,0:T(8,128)S(1)} copy-done((f32[1,384,1536]{2,1,0:T(8,128)S(1)}, f32[1,384,1536]{2,1,0:T(8,128)}, u32[]{:S(2)}) %copy-start.4) | copy-done | bytes 2359320
  68.6 7.2 %shard_map.113 = (f32[1,384,1536]{2,1,0:T(8,128)}, f32[1,384,1536]{2,1,0:T(8,128)}) custom-call(f32[2]{0:T(128)S(1)} %pad_maximum_fusion.3.scal, f32[1,384,1536]{2,1,0:T(8,128)S(1)} %copy-done, f32[1,384,1536]{2,1,0:T(8,128)S(1)} %copy-done, f32[1,384,1536]{2,1,0:T(8,128)S(1)} %copy-done, f32[1,384,1536]{2,1,0:T(8,128)S(1)} %copy-done.4, ...), custom_call_target="tpu_custom_call" | custom-call | flops 29491200 | bytes 14155776 | tf_op jit(solution)/shard_map/pallas_call | solution.py:132
  75.8 5.5 %collective-permute-done.2.far = f32[1,384,1536]{2,1,0:T(8,128)} collective-permute-done((f32[1,384,1536]{2,1,0:T(8,128)}, f32[1,384,1536]{2,1,0:T(8,128)}, u32[]{:S(2)}, u32[]{:S(2)}) %collective-permute-start.2) | collective-permute-done | bytes 2359328 | tf_op jit(solution)/shard_map/ppermute | solution.py:196
  81.3 4.6 %shard_map.114 = f32[1,384,1536]{2,1,0:T(8,128)} custom-call(f32[2]{0:T(128)S(1)} %pad_maximum_fusion.3.scal, f32[1,384,1536]{2,1,0:T(8,128)} %get-tuple-element.16.base, f32[1,384,1536]{2,1,0:T(8,128)} %collective-permute-done.2.far, f32[1,384,1536]{2,1,0:T(8,128)S(1)} %copy-done, f32[384,3]{1,0:T(8,128)S(1)} %copy.24.coef), custom_call_target="tpu_custom_call", output_to_operand_aliasing={{}: (1, {})} | custom-call | flops 5898240 | bytes 9437184 | tf_op jit(solution)/shard_map/pallas_call | solution.py:166
  85.9 14.4 %collective-permute-done.3.far = f32[1,288,1536]{2,1,0:T(8,128)} collective-permute-done((f32[1,288,1536]{2,1,0:T(8,128)}, f32[1,288,1536]{2,1,0:T(8,128)}, u32[]{:S(2)}, u32[]{:S(2)}) %collective-permute-start.3) | collective-permute-done | bytes 1769504 | tf_op jit(solution)/shard_map/ppermute | solution.py:217
  100.3 4.2 %shard_map.115.base = f32[1,384,1536]{2,1,0:T(8,128)} custom-call(f32[2]{0:T(128)S(1)} %pad_maximum_fusion.3.scal, f32[1,384,1536]{2,1,0:T(8,128)} %get-tuple-element.17.base, f32[1,288,1536]{2,1,0:T(8,128)} %collective-permute-done.3.far, f32[384,3]{1,0:T(8,128)S(1)} %copy.24.coef), custom_call_target="tpu_custom_call", output_to_operand_aliasing={{}: (1, {})} | custom-call | flops 4423680 | bytes 7077888 | tf_op jit(solution)/shard_map/pallas_call | solution.py:166
  104.5 0.4 collective-permute-done.4.far
  104.9 2.0 %shard_map.116 = f32[1,384,1536]{2,1,0:T(8,128)} custom-call(f32[2]{0:T(128)S(1)} %pad_maximum_fusion.3.scal, f32[1,384,1536]{2,1,0:T(8,128)} %shard_map.115.base, f32[1,72,1536]{2,1,0:T(8,128)S(1)} %collective-permute-done.4.far, f32[384,3]{1,0:T(8,128)S(1)} %copy.24.coef), custom_call_target="tpu_custom_call", output_to_operand_aliasing={{}: (1, {})} | custom-call | flops 1105920 | bytes 1769472 | tf_op jit(solution)/shard_map/pallas_call | solution.py:166
  106.8 0.0 collective-permute-done.10
  106.8 2.2 %add_dynamic-update-slice_fusion = f32[1,384,1536]{2,1,0:T(8,128)} fusion(f32[1,384,1536]{2,1,0:T(8,128)} %shard_map.116, f32[1,24,1536]{2,1,0:T(8,128)S(1)} %collective-permute-done.10, f32[24]{0:T(128)S(1)} %slice.40, f32[]{:T(128)S(6)} %mul.53, f32[]{:T(128)} %fusion.1), kind=kLoop, calls=%fused_computation | loop fusion | flops 258048 | bytes 442980 | tf_op jit(solution)/shard_map/dynamic_update_slice | solution.py:240
  (27 shorter events, 0.1 us)
Async XLA Ops:
  0.6 22.7 %copy-start.10 = (f32[3]{0:T(128)S(1)}, f32[3]{0:T(128)}, u32[]{:S(2)}) copy-start(f32[3]{0:T(128)} %constant.52) | copy-start | bytes 40
  0.6 24.2 %copy-start = (f32[1,384,1536]{2,1,0:T(8,128)S(1)}, f32[1,384,1536]{2,1,0:T(8,128)}, u32[]{:S(2)}) copy-start(f32[1,384,1536]{2,1,0:T(8,128)} %state.1) | copy-start | bytes 7077892
  0.7 14.3 %copy-start.6 = (f32[256]{0:T(256)S(1)}, f32[256]{0:T(256)}, u32[]{:S(2)}) copy-start(f32[256]{0:T(256)} %param.11) | copy-start | bytes 3076
  0.7 14.3 %copy-start.5 = (s32[1,1536]{1,0:T(1,128)S(1)}, s32[1,1536]{1,0:T(1,128)}, u32[]{:S(2)}) copy-start(s32[1,1536]{1,0:T(1,128)} %ids.1) | copy-start | bytes 18436
  0.7 21.4 %copy-start.7 = (f32[384]{0:T(512)S(1)}, f32[384]{0:T(512)}, u32[]{:S(2)}) copy-start(f32[384]{0:T(512)} %param.15) | copy-start | bytes 4612
  0.7 22.6 %copy-start.9 = (f32[384]{0:T(512)S(1)}, f32[384]{0:T(512)}, u32[]{:S(2)}) copy-start(f32[384]{0:T(512)} %param.14) | copy-start | bytes 4612
  0.7 22.6 %copy-start.8 = (f32[384]{0:T(512)S(1)}, f32[384]{0:T(512)}, u32[]{:S(2)}) copy-start(f32[384]{0:T(512)} %param.16) | copy-start | bytes 4612
  0.7 7.4 %collective-permute-start = (f32[1,384,1536]{2,1,0:T(8,128)}, f32[1,384,1536]{2,1,0:T(8,128)S(1)}, u32[]{:S(2)}, u32[]{:S(2)}) collective-permute-start(f32[1,384,1536]{2,1,0:T(8,128)} %state.1), channel_id=1, source_target_pairs={{0,1},{1,0},{2,3},{3,2},{4,5},{5,4},{6,7},{7,6},{8,9},{9,8},{10,11... | collective-permute-start | bytes 7077896 | tf_op jit(solution)/shard_map/ppermute | solution.py:198
  0.8 64.4 %collective-permute-start.1 = (f32[1,384,1536]{2,1,0:T(8,128)}, f32[1,384,1536]{2,1,0:T(8,128)}, u32[]{:S(2)}, u32[]{:S(2)}) collective-permute-start(f32[1,384,1536]{2,1,0:T(8,128)} %c_down.1), channel_id=1, source_target_pairs={{0,1},{1,0},{2,3},{3,2},{4,5},{5,4},{6,7},{7,6},{8,9},{9,8},{10,11... | collective-permute-start | bytes 7077896 | tf_op jit(solution)/shard_map/ppermute | solution.py:197
  1.3 80.0 %collective-permute-start.2 = (f32[1,384,1536]{2,1,0:T(8,128)}, f32[1,384,1536]{2,1,0:T(8,128)}, u32[]{:S(2)}, u32[]{:S(2)}) collective-permute-start(f32[1,384,1536]{2,1,0:T(8,128)} %c_down.1), channel_id=1, source_target_pairs={{0,15},{1,2},{2,1},{3,4},{4,3},{5,6},{6,5},{7,8},{8,7},{9,10},{10,... | collective-permute-start | bytes 7077896 | tf_op jit(solution)/shard_map/ppermute | solution.py:196
  8.1 1.4 %copy-start.3 = (f32[1,384,1536]{2,1,0:T(8,128)}, f32[1,384,1536]{2,1,0:T(8,128)S(1)}, u32[]{:S(2)}) copy-start(f32[1,384,1536]{2,1,0:T(8,128)S(1)} %collective-permute-done.q_near) | copy-start | bytes 7077892
  12.4 87.9 %collective-permute-start.3 = (f32[1,288,1536]{2,1,0:T(8,128)}, f32[1,288,1536]{2,1,0:T(8,128)}, u32[]{:S(2)}, u32[]{:S(2)}) collective-permute-start(f32[1,288,1536]{2,1,0:T(8,128)} %slice.36), channel_id=1, source_target_pairs={{0,15},{1,2},{2,1},{3,4},{4,3},{5,6},{6,5},{7,8},{8,7},{9,10},{10,... | collective-permute-start | bytes 5308424 | tf_op jit(solution)/shard_map/ppermute | solution.py:217
  15.0 1.7 %copy-start.1 = (f32[1,384,1536]{2,1,0:T(8,128)S(1)}, f32[1,384,1536]{2,1,0:T(8,128)}, u32[]{:S(2)}) copy-start(f32[1,384,1536]{2,1,0:T(8,128)} %c_down.1) | copy-start | bytes 7077892
  18.9 5.9 %collective-permute-start.5 = (f32[1,256]{1,0:T(1,128)S(1)}, f32[1,256]{1,0:T(1,128)S(1)}, u32[]{:S(2)}, u32[]{:S(2)}) collective-permute-start(f32[1,256]{1,0:T(1,128)S(1)} %get-tuple-element.19), channel_id=1, source_target_pairs={{0,1},{1,0},{2,3},{3,2},{4,5},{5,4},{6,7},{7,6},{8,9},{9,8},{10,11... | collective-permute-start | bytes 3080 | tf_op jit(solution)/shard_map/ppermute | solution.py:207
  24.8 3.0 %collective-permute-start.6 = (f32[1,256]{1,0:T(1,128)S(1)}, f32[1,256]{1,0:T(1,128)S(1)}, u32[]{:S(2)}, u32[]{:S(2)}) collective-permute-start(f32[1,256]{1,0:T(1,128)S(1)} %add.35), channel_id=1, source_target_pairs={{0,4},{1,5},{2,6},{3,7},{4,0},{5,1},{6,2},{7,3},{8,12},{9,13},{10,... | collective-permute-start | bytes 3080 | tf_op jit(solution)/shard_map/ppermute | solution.py:207
  25.7 79.2 %collective-permute-start.4 = (f32[1,72,1536]{2,1,0:T(8,128)}, f32[1,72,1536]{2,1,0:T(8,128)S(1)}, u32[]{:S(2)}, u32[]{:S(2)}) collective-permute-start(f32[1,72,1536]{2,1,0:T(8,128)} %slice.37), channel_id=1, source_target_pairs={{0,15},{1,2},{2,1},{3,4},{4,3},{5,6},{6,5},{7,8},{8,7},{9,10},{10,... | collective-permute-start | bytes 1327112 | tf_op jit(solution)/shard_map/ppermute | solution.py:217
  27.7 3.8 %collective-permute-start.7 = (f32[1,256]{1,0:T(1,128)S(1)}, f32[1,256]{1,0:T(1,128)S(1)}, u32[]{:S(2)}, u32[]{:S(2)}) collective-permute-start(f32[1,256]{1,0:T(1,128)S(1)} %add.36), channel_id=1, source_target_pairs={{0,8},{1,9},{2,10},{3,11},{4,12},{5,13},{6,14},{7,15},{8,0},{9,1},... | collective-permute-start | bytes 3080 | tf_op jit(solution)/shard_map/ppermute | solution.py:207
  31.5 1.3 %collective-permute-start.8 = (f32[1,256]{1,0:T(1,128)S(1)}, f32[1,256]{1,0:T(1,128)S(1)}, u32[]{:S(2)}, u32[]{:S(2)}) collective-permute-start(f32[1,256]{1,0:T(1,128)S(1)} %add.37), channel_id=1, source_target_pairs={{0,3},{3,0},{4,7},{7,4},{8,11},{11,8},{12,15},{15,12},{16,19},{19,... | collective-permute-start | bytes 3080 | tf_op jit(solution)/shard_map/ppermute | solution.py:209
  32.8 31.5 %collective-permute-start.9 = (f32[1,256]{1,0:T(1,128)S(1)}, f32[1,256]{1,0:T(1,128)S(1)}, u32[]{:S(2)}, u32[]{:S(2)}) collective-permute-start(f32[1,256]{1,0:T(1,128)S(1)} %add.38), channel_id=1, source_target_pairs={{0,1},{3,2},{4,5},{7,6},{8,9},{11,10},{12,13},{15,14},{16,17},{19,... | collective-permute-start | bytes 3080 | tf_op jit(solution)/shard_map/ppermute | solution.py:211
  64.3 42.6 %collective-permute-start.10 = (f32[1,24,1536]{2,1,0:T(8,128)S(1)}, f32[1,24,1536]{2,1,0:T(8,128)S(1)}, u32[]{:S(2)}, u32[]{:S(2)}) collective-permute-start(f32[1,24,1536]{2,1,0:T(8,128)S(1)} %slice.39), channel_id=1, source_target_pairs={{0,15},{1,2},{2,1},{3,4},{4,3},{5,6},{6,5},{7,8},{8,7},{9,10},{10,... | collective-permute-start | bytes 442376 | tf_op jit(solution)/shard_map/ppermute | solution.py:217
  65.2 1.7 %copy-start.2 = (f32[1,384,1536]{2,1,0:T(8,128)S(1)}, f32[1,384,1536]{2,1,0:T(8,128)}, u32[]{:S(2)}) copy-start(f32[1,384,1536]{2,1,0:T(8,128)} %c_down.1) | copy-start | bytes 7077892
  66.9 1.7 %copy-start.4 = (f32[1,384,1536]{2,1,0:T(8,128)S(1)}, f32[1,384,1536]{2,1,0:T(8,128)}, u32[]{:S(2)}) copy-start(f32[1,384,1536]{2,1,0:T(8,128)} %copy-done.3) | copy-start | bytes 7077892
